TPU v7x, 128 devices: a whole 4x4x4 slice. The times are simulated.
128 devices in a mesh: particle: 128 (over y, z, x, core).
Axes of the slice: x: 4, y: 4, z: 4, core: 2. Of those that a mesh axis runs over, the one named last changes fastest.
Arguments:
- x_prev: bfloat16 [65536, 512], P('particle'), may hold values from -6 to 6
- anc_owner: int32 [65536, 1], P('particle'), may hold values from 0 to 127; in each aligned block of 512 rows (0 to 511, 512 to 1023, ...) at most 8 rows name the same one
- anc_row: int32 [65536], P('particle'), may hold values from 0 to 511
- noise: bfloat16 [65536, 512], P('particle'), may hold values from -6 to 6
- g_new: bfloat16 [65536, 512], P('particle'), may hold values from -6 to 6
- obs: bfloat16 [65536, 128], P('particle'), may hold values from -64 to 64
- w1: bfloat16 [512, 1024], replicated, may hold values from -0.25 to 0.25
- b1: float32 [1024], replicated, may hold values from -3 to 3
- w2: bfloat16 [1024, 512], replicated, may hold values from -0.1875 to 0.1875
- b2: float32 [512], replicated, may hold values from -3 to 3
- c_obs: bfloat16 [512, 128], replicated, may hold values from -0.25 to 0.25
- inv_scale: float32 [128], replicated, may hold values from 0.04 to 0.12
- sigma: float32 [512], replicated, may hold values from 0.1 to 0.5
Outputs:
- d_prev: float32 [65536, 512], P('particle')
- d_w1: float32 [512, 1024], replicated
- d_b1: float32 [1024], replicated
- d_w2: float32 [1024, 512], replicated
- d_b2: float32 [512], replicated
- d_c: float32 [512, 128], replicated
- d_sigma: float32 [512], replicated
Inputs may be any that keep to these rules, and one draw needn't show every extreme that they name: `anc_owner`: within the 512 rows of one device no device index appears more than 8 times, and in some device's rows one appears exactly 8 times.
All inputs are finite; a program needn't handle non-finite values.
Results may differ from a plain program's by a relative error of at most 0.0056.
Values may be sent and summed in bfloat16 or wider, within the bound.
A program may use at most 64 MiB of HBM per device.

v0:
```python
import jax
import jax.numpy as jnp
from jax import lax
from jax.sharding import PartitionSpec as P

HEUN = 0.25


def tdot(left, right):
    return lax.dot_general(
        left, right, (((0,), (0,)), ((), ())), preferred_element_type=jnp.float32
    )


def rdot(left, right):
    return lax.dot_general(
        left, right, (((1,), (1,)), ((), ())), preferred_element_type=jnp.float32
    )


def forward(x_start, noise, obs, w1, b1, w2, b2, c_obs, inv_scale, sigma):
    t_zero = jnp.tanh(jnp.dot(x_start, w1, preferred_element_type=jnp.float32) + b1)
    a_zero = t_zero.astype(jnp.bfloat16)
    f_zero = jnp.dot(a_zero, w2, preferred_element_type=jnp.float32) + b2
    kick = sigma * noise.astype(jnp.float32)
    x_pred = (x_start.astype(jnp.float32) + HEUN * f_zero + kick).astype(jnp.bfloat16)
    t_one = jnp.tanh(jnp.dot(x_pred, w1, preferred_element_type=jnp.float32) + b1)
    a_one = t_one.astype(jnp.bfloat16)
    f_one = jnp.dot(a_one, w2, preferred_element_type=jnp.float32) + b2
    x_next = x_start.astype(jnp.float32) + 0.5 * HEUN * (f_zero + f_one) + kick
    x_round = x_next.astype(jnp.bfloat16)
    resid = (
        obs.astype(jnp.float32) - jnp.dot(x_round, c_obs, preferred_element_type=jnp.float32)
    ) * inv_scale
    loglik = -0.5 * jnp.sum(resid * resid, axis=1)
    return (loglik, (t_zero, a_zero, x_pred, t_one, a_one, x_round, resid))


def backward(x_start, noise, g_new, weight_q, saved, w1, w2, c_obs, inv_scale):
    t_zero, a_zero, x_pred, t_one, a_one, x_round, resid = saved
    dmean = (weight_q[:, None] * resid * inv_scale).astype(jnp.bfloat16)
    gxn = g_new.astype(jnp.float32) + rdot(dmean, c_obs)
    d_c = tdot(x_round, dmean)
    gf_one = 0.5 * HEUN * gxn
    gf_one_b = gf_one.astype(jnp.bfloat16)
    gp_one = rdot(gf_one_b, w2) * (1.0 - t_one * t_one)
    gp_one_b = gp_one.astype(jnp.bfloat16)
    gxp = rdot(gp_one_b, w1)
    gf_zero = 0.5 * HEUN * gxn + HEUN * gxp
    gf_zero_b = gf_zero.astype(jnp.bfloat16)
    gp_zero = rdot(gf_zero_b, w2) * (1.0 - t_zero * t_zero)
    gp_zero_b = gp_zero.astype(jnp.bfloat16)
    gx_zero = gxn + gxp + rdot(gp_zero_b, w1)
    d_w2 = tdot(a_one, gf_one_b) + tdot(a_zero, gf_zero_b)
    d_b2 = jnp.sum(gf_one + gf_zero, axis=0)
    d_w1 = tdot(x_pred, gp_one_b) + tdot(x_start, gp_zero_b)
    d_b1 = jnp.sum(gp_one + gp_zero, axis=0)
    d_sigma = jnp.sum((gxn + gxp) * noise.astype(jnp.float32), axis=0)
    return (gx_zero, (d_w1, d_b1, d_w2, d_b2, d_c, d_sigma))


def normalize(loglik, live, count):
    masked = jnp.where(live, loglik, -1e30)
    local_peak = jnp.max(masked)
    peak = lax.pmax(local_peak, "particle")
    local_total = jnp.sum(jnp.where(live, jnp.exp(masked - peak), 0.0))
    total = lax.psum(local_total, "particle")
    return jnp.where(live, jnp.exp(masked - peak), 0.0) / total * count


def sum_grads(grads):
    summed = lax.psum((grads[0], grads[1], grads[2], grads[3], grads[4], grads[5]), "particle")
    return (summed[0], summed[1], summed[2], summed[3], summed[4], summed[5])


def per_device(
    x_prev, anc_owner, anc_row, noise, g_new, obs, w1, b1, w2, b2, c_obs, inv_scale, sigma
):
    rows = x_prev.shape[0]
    width = x_prev.shape[1]
    devices = lax.axis_size("particle")
    most = 2 * rows // devices
    count = float(rows * devices)
    owner = anc_owner[:, 0]
    onehot = (owner[:, None] == jnp.arange(devices, dtype=jnp.int32)[None, :]).astype(jnp.int32)
    before = jnp.cumsum(onehot, axis=0) - onehot
    slot = jnp.sum(before * onehot, axis=1)
    flat = owner * most + slot
    wanted = jnp.full((devices * most,), -1, jnp.int32).at[flat].set(anc_row).reshape(devices, most)
    incoming = lax.all_to_all(wanted, "particle", split_axis=0, concat_axis=0, tiled=True).reshape(
        devices * most
    )
    live_in = incoming >= 0
    safe = jnp.where(live_in, incoming, 0)
    target = jnp.where(live_in, incoming, rows)
    sent_rows = x_prev[safe].reshape(devices, most, width)
    fetched = lax.all_to_all(
        sent_rows, "particle", split_axis=0, concat_axis=0, tiled=True
    ).reshape(devices * most, width)
    x_start = fetched[flat]
    loglik, saved = forward(x_start, noise, obs, w1, b1, w2, b2, c_obs, inv_scale, sigma)
    weight_q = normalize(loglik, jnp.ones(loglik.shape, jnp.bool_), count)
    gx_zero, grads = backward(x_start, noise, g_new, weight_q, saved, w1, w2, c_obs, inv_scale)
    returned = (
        jnp.zeros((devices * most, width), jnp.float32)
        .at[flat]
        .set(gx_zero)
        .reshape(devices, most, width)
    )
    arrived = lax.all_to_all(returned, "particle", split_axis=0, concat_axis=0, tiled=True).reshape(
        devices * most, width
    )
    d_prev = jnp.zeros((rows, width), jnp.float32).at[target].add(arrived, mode="drop")
    d_w1, d_b1, d_w2, d_b2, d_c, d_sigma = sum_grads(grads)
    return (d_prev, d_w1, d_b1, d_w2, d_b2, d_c, d_sigma)


def solution(mesh):
    return jax.shard_map(
        per_device,
        mesh=mesh,
        in_specs=(
            P("particle", None),
            P("particle", None),
            P("particle"),
            P("particle", None),
            P("particle", None),
            P("particle", None),
            P(),
            P(),
            P(),
            P(),
            P(),
            P(),
            P(),
        ),
        out_specs=(P("particle", None), P(), P(), P(), P(), P(), P()),
        check_vma=False,
    )
```

profile of v0, /device:TPU:1, one launch (start us, length us, event | category | flops | bytes accessed | tf_op | source)
XLA Modules:
  0.0 397.8 jit_solution(18345606671477921139)
XLA Ops:
  7.2 0.9 copy.25
  8.1 0.2 fusion.30
  8.4 0.9 fusion.29
  9.3 0.7 compare_select_fusion.4
  10.0 2.6 scatter_custom_fusion
  12.6 0.1 all_to_all.12
  12.7 20.8 %all_to_all.19 = s32[128,1,8]{2,1,0:T(1,128)S(1)} all-to-all(s32[128,1,8]{2,1,0:T(1,128)S(1)} %bitcast.53), channel_id=1, replica_groups=mesh['particle'=128] {'particle'}, dimensions={0} | all-to-all | bytes 8192 | tf_op jit(solution)/shard_map/all_to_all | solution.py:90
  33.5 0.5 broadcast.145
  34.0 0.8 reduce.3
  34.8 0.1 reshape.114
  35.0 5.1 %gather_fusion = bf16[1024,512]{1,0:T(8,128)(2,1)} fusion(bf16[512,512]{1,0:T(8,128)(2,1)S(1)} %copy-done.1, s32[1024]{0:T(1024)S(1)} %broadcast_clamp_fusion), kind=kCustom, calls=%fused_computation | custom fusion | bytes 2101248 | tf_op jit(solution)/shard_map/gather | solution.py:96
  40.1 4.6 %all-to-all-start.1 = ((bf16[128,8,512]{2,1,0:T(8,128)(2,1)}), bf16[128,8,512]{2,1,0:T(8,128)(2,1)S(1)}, u32[]{:S(2)}, u32[]{:S(2)}) async-start(bf16[128,8,512]{2,1,0:T(8,128)(2,1)} %bitcast.50), calls=%async_computation.1 | async-start | bytes 2097152 | tf_op jit(solution)/shard_map/all_to_all | solution.py:97
  44.7 0.8 copy.28
  45.5 18.5 %all-to-all-done.1 = bf16[128,8,512]{2,1,0:T(8,128)(2,1)S(1)} async-done(((bf16[128,8,512]{2,1,0:T(8,128)(2,1)}), bf16[128,8,512]{2,1,0:T(8,128)(2,1)S(1)}, u32[]{:S(2)}, u32[]{:S(2)}) %all-to-all-start.1) | async-done | bytes 1048608 | tf_op jit(solution)/shard_map/all_to_all | solution.py:97
  64.0 2.6 gather_fusion.1
  66.7 1.8 fusion.39
  68.6 0.8 fusion.11
  69.5 0.5 copy-done.2
  69.9 0.8 copy-done.10
  70.7 0.7 fusion.40
  71.5 0.9 fusion.8
  72.4 0.4 copy-done.4
  72.8 0.3 multiply_reduce_fusion
  73.1 0.6 multiply_reduce_fusion.1
  73.7 62.5 %pmax.7 = f32[]{:T(128)} all-reduce(f32[]{:T(128)} %multiply_reduce_fusion.1), channel_id=1, replica_groups=mesh['particle'=128] {'particle'}, use_global_device_ids=true, to_apply=%region_6.7 | all-reduce | flops 1 | bytes 8 | tf_op jit(solution)/shard_map/pmax | solution.py:65
  136.2 1.3 fusion.35
  137.5 63.1 %psum.49 = f32[]{:T(128)} all-reduce(f32[]{:T(128)} %fusion.35), channel_id=1, replica_groups=mesh['particle'=128] {'particle'}, use_global_device_ids=true, to_apply=%region_8.9 | all-reduce | flops 1 | bytes 8 | tf_op jit(solution)/shard_map/psum | solution.py:67
  200.5 1.4 divide_multiply_fusion
  202.0 1.1 fusion.38
  203.1 1.4 convolution_add_fusion.3
  204.5 0.8 subtract_multiply_fusion.1
  205.3 0.8 fusion.23
  206.1 0.2 copy-done.11
  206.4 0.8 fusion.18
  207.1 0.3 copy-done.16
  207.4 1.9 fusion.12
  209.3 0.9 add_reduce_fusion
  210.2 2.1 convolution_add_fusion
  212.3 2.0 convolution_add_fusion.1
  214.4 3.3 convolution_add_fusion.2
  217.7 4.3 %scatter_custom_fusion.1 = f32[1024,512]{1,0:T(8,128)} fusion(s32[512]{0:T(512)S(1)} %bitcast.61, f32[512,512]{1,0:T(8,128)} %convolution_add_fusion.2, f32[]{:T(128)} %constant.12.clone.1), kind=kCustom, calls=%fused_computation.35 | custom fusion | bytes 2097664 | tf_op jit(solution)/shard_map/scatter | solution.py:107
  222.0 5.0 %all-to-all-start.2 = ((f32[128,8,512]{2,1,0:T(8,128)}), f32[128,8,512]{2,1,0:T(8,128)S(1)}, u32[]{:S(2)}, u32[]{:S(2)}) async-start(f32[128,8,512]{2,1,0:T(8,128)} %bitcast.49), calls=%async_computation.2 | async-start | bytes 4194304 | tf_op jit(solution)/shard_map/all_to_all | solution.py:110
  227.0 85.0 %all-reduce = (f32[1024]{0:T(1024)}, f32[512]{0:T(512)}, f32[512]{0:T(512)}) all-reduce(f32[1024]{0:T(1024)S(1)} %get-tuple-element.23, f32[512]{0:T(512)S(1)} %get-tuple-element.8, f32[512]{0:T(512)S(1)} %get-tuple-element.7), channel_id=1, replica_groups=mesh['particle'=128] {'particle'}, use_global_device_ids=true, to_apply=%region_13.14 | all-reduce | flops 2048 | bytes 16384 | tf_op jit(solution)/shard_map/psum | solution.py:72
  312.0 7.7 %scatter_custom_fusion.2 = f32[512,512]{1,0:T(8,128)} fusion(s32[1024]{0:T(1024)S(1)} %bitcast.62, f32[128,8,512]{2,1,0:T(8,128)S(1)} %all-to-all-done.2, f32[]{:T(128)} %constant.12.clone.1), kind=kCustom, calls=%fused_computation.5 | custom fusion | flops 524288 | bytes 3145732 | tf_op jit(solution)/shard_map/scatter-add | solution.py:113
  319.7 66.0 %all-reduce.4.cloned.1.call-done = (f32[512,1024]{1,0:T(8,128)}, f32[1024,512]{1,0:T(8,128)}, f32[512,128]{1,0:T(8,128)}) async-done(((f32[512,1024]{1,0:T(8,128)}, f32[1024,512]{1,0:T(8,128)}, f32[512,128]{1,0:T(8,128)}), (f32[512,1024]{1,0:T(8,128)}, f32[1024,512]{1,0:T(8,128)}, f32[512,128]{1,0:T(8,128)})) %all-reduce.4.cloned.1.call-update) | async-done | bytes 4456464 | tf_op jit(solution)/shard_map/psum | solution.py:72
  385.6 3.3 copy.32
  388.9 1.3 copy.33
  390.3 0.7 copy.34
  (53 shorter events, 0.3 us)
Async XLA Ops:
  7.2 61.4 %copy-start = (bf16[1024,512]{1,0:T(8,128)(2,1)S(1)}, bf16[1024,512]{1,0:T(8,128)(2,1)}, u32[]{:S(2)}) copy-start(bf16[1024,512]{1,0:T(8,128)(2,1)} %param.21) | copy-start | bytes 3145732
  7.2 27.8 %copy-start.1 = (bf16[512,512]{1,0:T(8,128)(2,1)S(1)}, bf16[512,512]{1,0:T(8,128)(2,1)}, u32[]{:S(2)}) copy-start(bf16[512,512]{1,0:T(8,128)(2,1)} %param.13) | copy-start | bytes 1572868
  40.1 4.7 %copy-start.18 = (bf16[512,128]{1,0:T(8,128)(2,1)S(1)}, bf16[512,128]{1,0:T(8,128)(2,1)}, u32[]{:S(2)}) copy-start(bf16[512,128]{1,0:T(8,128)(2,1)} %param.18) | copy-start | bytes 393220
  40.1 24.0 %all-to-all-start.1 = ((bf16[128,8,512]{2,1,0:T(8,128)(2,1)}), bf16[128,8,512]{2,1,0:T(8,128)(2,1)S(1)}, u32[]{:S(2)}, u32[]{:S(2)}) async-start(bf16[128,8,512]{2,1,0:T(8,128)(2,1)} %bitcast.50), calls=%async_computation.1 | async-start | bytes 2097152 | tf_op jit(solution)/shard_map/all_to_all | solution.py:97
  44.7 340.9 %all-reduce.4.cloned.1.call-start = ((), (), s32[]{:S(2)}) async-start(), calls=%async_computation.3 | async-start | bytes 8912896 | tf_op jit(solution)/shard_map/psum | solution.py:72
  64.0 2.6 copy-start.6
  66.7 1.9 copy-start.8
  66.7 1.9 copy-start.15
  66.7 1.9 copy-start.19
  66.7 1.9 copy-start.21
  66.7 1.9 copy-start.22
  68.6 1.3 copy-start.2
  69.9 0.8 copy-start.10
  71.4 1.3 copy-start.4
  71.5 1.3 copy-start.13
  71.5 1.3 copy-start.14
  71.5 1.3 copy-start.20
  200.5 4.0 %copy-start.5 = (f32[512,1024]{1,0:T(8,128)S(1)}, f32[512,1024]{1,0:T(8,128)}, u32[]{:S(2)}) copy-start(f32[512,1024]{1,0:T(8,128)} %copy-done.4) | copy-start | bytes 6291460
  205.3 1.0 copy-start.11
  206.4 1.0 copy-start.16
  207.4 1.9 copy-start.3
  210.2 2.1 copy-start.7
  210.2 2.1 copy-start.9
  222.0 90.0 %all-to-all-start.2 = ((f32[128,8,512]{2,1,0:T(8,128)}), f32[128,8,512]{2,1,0:T(8,128)S(1)}, u32[]{:S(2)}, u32[]{:S(2)}) async-start(f32[128,8,512]{2,1,0:T(8,128)} %bitcast.49), calls=%async_computation.2 | async-start | bytes 4194304 | tf_op jit(solution)/shard_map/all_to_all | solution.py:110
  385.6 3.3 copy-start.12
  388.9 1.3 copy-start.17
Sparse Core Ops, SparseCore 0:
  214.5 171.0 all-reduce.3
where the time goes:
time: 399 us; the launch traced here: 398 us
  blocking collectives  231 us (58%)
  waiting for transfers between devices  84.5 us (21%)
  local copies, waits for them, and re-layouts  24.6 us (6%)
  matrix products  19.7 us (5%)
  between operations  14.4 us (4%)
  other arithmetic  13.7 us (3%)
  starting transfers between devices  9.63 us (2%)
    psum x1, blocking collectives, sum_grads(): lax.psum((grads[0], grads[1], grads[2], grads[3], grads[4], grads[5]), 'p...  85 us
    psum x1, waiting for transfers between devices, sum_grads(): lax.psum((grads[0], grads[1], grads[2], grads[3], grads[4], grads[5]), 'p...  66 us
    psum x1, blocking collectives, normalize(): total = lax.psum(local_total, 'particle')  63.1 us
    pmax x1, blocking collectives, normalize(): peak = lax.pmax(local_peak, 'particle')  62.5 us
    all_to_all x1, blocking collectives, per_device(): lax.all_to_all(wanted, 'particle', split_axis=0, concat_axis=0, tiled=True)  20.8 us
    all_to_all x1, waiting for transfers between devices, per_device(): lax.all_to_all(sent_rows, 'particle', split_axis=0, concat_axis=0, tiled=...  18.5 us
    unnamed x51, local copies, waits for them, and re-layouts  8.35 us
    dot_general x5, matrix products, rdot(): lax.dot_general(left, right, (((1,), (1,)), ((), ())), preferred_element_...  8.25 us
  transfers between devices with their start and end apart: 3, of which 2 were waited for; matrix products, arithmetic and copies ran while one was open for 4% of the time, Pallas kernels for 0%

commit v1 on v0

v1 whole, which is shorter than its diff:
```python
import functools

import jax
import jax.numpy as jnp
from jax import lax
from jax.experimental import pallas as pl
from jax.experimental.pallas import tpu as pltpu
from jax.sharding import PartitionSpec as P

MESH = pl.DeviceIdType.MESH
HEUN = 0.25
F32 = jnp.float32
BF16 = jnp.bfloat16
I32 = jnp.int32
MOST = 8
LOGSTEP = 65536.0
TOP = 32767.0


def nn(left, right):
    return jnp.dot(left, right, preferred_element_type=F32)


def nt(left, right):
    return lax.dot_general(left, right, (((1,), (1,)), ((), ())), preferred_element_type=F32)


def tn(left, right):
    return lax.dot_general(left, right, (((0,), (0,)), ((), ())), preferred_element_type=F32)


def iota(shape, dim):
    return lax.broadcasted_iota(I32, shape, dim)


def split(value):
    high = value.astype(BF16)
    return high, (value - high.astype(F32)).astype(BF16)


def encode(value):
    peak = jnp.max(jnp.max(jnp.abs(value), axis=2, keepdims=True), axis=1, keepdims=True)
    level = jnp.ceil(jnp.log(jnp.maximum(peak, 1e-30)) * LOGSTEP).astype(I32)
    scale = TOP * jnp.exp(level.astype(F32) * (-1.0 / LOGSTEP))
    code = jnp.round(value * scale).astype(I32)
    return code, jnp.broadcast_to(level, (value.shape[0], 1, 128))


def pack(low, high):
    return jnp.bitwise_or(jnp.left_shift(high, 16), jnp.bitwise_and(low, 0xFFFF))


def unpack(word):
    low = jnp.right_shift(jnp.left_shift(word, 16), 16)
    return low.astype(F32), jnp.right_shift(word, 16).astype(F32)


def encode_wide(value):
    code, level = encode(value)
    word = pack(code[:, :, :256], code[:, :, 256:])
    return jnp.concatenate([word[:, :, :128], word[:, :, 128:]], axis=1), level


def unscale(level):
    return jnp.exp(level.astype(F32) * (1.0 / LOGSTEP)) * (1.0 / TOP)


def decode_wide(word, level):
    scale = unscale(level)
    low0, high0 = unpack(word[:, :8])
    low1, high1 = unpack(word[:, 8:])
    return jnp.concatenate([low0 * scale, low1 * scale, high0 * scale, high1 * scale], axis=2)


def encode_slice(one, two, rest):
    word1, level1 = encode_wide(one)
    word2, level2 = encode_wide(two)
    code3, level3 = encode(rest)
    word3 = pack(code3[:, :4], code3[:, 4:])
    return jnp.concatenate([word1, word2, word3, level1, level2, level3, level3], axis=1)


def decode_slice(word):
    one = decode_wide(word[:, 0:16], word[:, 36:37])
    two = decode_wide(word[:, 16:32], word[:, 37:38])
    scale = unscale(word[:, 38:39])
    low, high = unpack(word[:, 32:36])
    return one, two, jnp.concatenate([low * scale, high * scale], axis=1)


def wanted_columns(table):
    shape = (1, MOST, 128)
    lane, sub = iota(shape, 2), iota(shape, 1)
    one = jnp.where((lane == sub) | (lane == sub + 2 * MOST), 1.0, 0.0)
    weight = jnp.where(lane == sub + MOST, 256.0, one)
    return jnp.sum(table * weight, axis=2, keepdims=True) - 1.0


def bytes_wait(ref, semaphore):
    pltpu.make_async_copy(ref, ref, semaphore).wait()


def main_kernel(
    devices,
    x_ref, owner_ref, row_ref, noise_ref, g_ref, obs_ref, w1_ref, b1_ref, w2_ref, b2_ref, c_ref, inv_ref, sigma_ref,
    inc_ref, arr_ref, all_ref,
    wtab, wrow, send_rows, recv_rows, norm_src, norm_tab, ret, xx, aa, gf, gp, u0, u1, xnb, f0s, gxs, dots,
    acc1, acc2, accx, in1, in2, inx, enc, got, fin,
    ssem, rsem,
):
    me = lax.axis_index("particle")
    rows, width = x_ref.shape
    hidden = w1_ref.shape[1]
    chips = devices // 2
    chip, core = lax.div(me, 2), lax.rem(me, 2)
    other = me + 1 - 2 * core

    barrier = pltpu.get_barrier_semaphore()

    def greet(k, carry):
        pl.semaphore_signal(barrier, inc=1, device_id=(lax.rem(me + k, devices),), device_id_type=MESH)
        return carry

    lax.fori_loop(1, devices, greet, 0)

    owner = owner_ref[...]
    row = row_ref[...]
    named = jnp.where(iota((devices, rows), 0) == owner, 1.0, 0.0)
    named_b = named.astype(BF16)
    earlier = jnp.where(iota((rows, rows), 0) < iota((rows, rows), 1), 1.0, 0.0).astype(BF16)
    slot = jnp.sum(nn(named_b, earlier) * named, axis=0, keepdims=True)
    part = iota((128, rows), 0)
    low = jnp.bitwise_and(row, 255).astype(F32)
    high = jnp.right_shift(row, 8).astype(F32)
    value = jnp.where(part < MOST, low, jnp.where(part < 2 * MOST, high, jnp.where(part < 3 * MOST, 1.0, 0.0)))
    value = jnp.where(jnp.bitwise_and(part, MOST - 1).astype(F32) == slot, value, 0.0)
    wrow[...] = nt(named_b, value.astype(BF16))

    def spread(d, carry):
        wtab[d] = wrow[pl.ds(d, 1), :]
        return carry

    lax.fori_loop(0, devices, spread, 0, unroll=8)
    eye = jnp.where(iota((rows, rows), 0) == iota((rows, rows), 1), 1.0, 0.0).astype(BF16)
    pair = jnp.where(part == 0, owner.astype(F32), jnp.where(part == 1, slot, 0.0)).astype(BF16)
    turned = nt(eye, pair)
    place = turned[:, 0:1] * (2 * MOST) + turned[:, 1:2]
    flat = owner * MOST + slot.astype(I32)

    pl.semaphore_wait(barrier, devices - 1)

    def exchange(stage, source, target, partner_block):
        def send(k, carry):
            d = lax.rem(me + k, devices)
            pltpu.make_async_remote_copy(
                src_ref=source.at[d] if partner_block else source.at[0],
                dst_ref=target.at[me],
                send_sem=ssem.at[stage],
                recv_sem=rsem.at[stage],
                device_id=(d,),
                device_id_type=MESH,
            ).start()
            return carry

        lax.fori_loop(1, devices, send, 0)

    def exchange_wait(stage, target):
        most = target.at[pl.ds(0, devices - 1)]
        bytes_wait(most, ssem.at[stage])
        bytes_wait(most, rsem.at[stage])

    exchange(0, wtab, inc_ref, True)
    inc_ref[me] = wtab[me]
    exchange_wait(0, inc_ref)

    group = 16

    def gather(i, carry):
        at = pl.multiple_of(i * group, group)
        column = wanted_columns(inc_ref[pl.ds(at, group)])
        onehot = jnp.where(column == iota((group, MOST, rows), 2).astype(F32), 1.0, 0.0)
        out = nn(onehot.reshape(group * MOST, rows).astype(BF16), x_ref[...])
        halves = jnp.concatenate(
            [out[:, : width // 2].reshape(group, MOST, width // 2), out[:, width // 2 :].reshape(group, MOST, width // 2)],
            axis=1,
        )
        send_rows[pl.ds(at, group)] = halves.astype(BF16)
        return carry

    lax.fori_loop(0, devices // group, gather, 0)
    exchange(1, send_rows, recv_rows, True)
    recv_rows[me] = send_rows[me]
    exchange_wait(1, recv_rows)

    def start(i, carry):
        left, right = carry
        at = pl.multiple_of(i * group, group)
        block = recv_rows[pl.ds(at, group)].reshape(group * 2 * MOST, width // 2)
        index = (iota((rows, group * 2 * MOST), 1) + at * (2 * MOST)).astype(F32)
        take_left = jnp.where(place == index, 1.0, 0.0).astype(BF16)
        take_right = jnp.where(place + MOST == index, 1.0, 0.0).astype(BF16)
        return left + nn(take_left, block), right + nn(take_right, block)

    none = jnp.zeros((rows, width // 2), F32)
    left, right = lax.fori_loop(0, devices // group, start, (none, none))
    xx[rows:, : width // 2] = left.astype(BF16)
    xx[rows:, width // 2 :] = right.astype(BF16)

    x0 = xx[rows:, :]
    block = 256
    for n in range(0, hidden, block):
        t = jnp.tanh(nn(x0, w1_ref[:, n : n + block]) + b1_ref[:, n : n + block])
        aa[rows:, n : n + block] = t.astype(BF16)
        u0[:, n : n + block] = 1.0 - t * t
    for n in range(0, width, block):
        cols = slice(n, n + block)
        f = nn(aa[rows:, :], w2_ref[:, cols]) + b2_ref[:, cols]
        kick = sigma_ref[:, cols] * noise_ref[:, cols].astype(F32)
        f0s[:, cols] = f
        xx[:rows, cols] = (xx[rows:, cols].astype(F32) + HEUN * f + kick).astype(BF16)
    xp = xx[:rows, :]
    for n in range(0, hidden, block):
        t = jnp.tanh(nn(xp, w1_ref[:, n : n + block]) + b1_ref[:, n : n + block])
        aa[:rows, n : n + block] = t.astype(BF16)
        u1[:, n : n + block] = 1.0 - t * t
    for n in range(0, width, block):
        cols = slice(n, n + block)
        f = nn(aa[:rows, :], w2_ref[:, cols]) + b2_ref[:, cols]
        kick = sigma_ref[:, cols] * noise_ref[:, cols].astype(F32)
        xn = xx[rows:, cols].astype(F32) + 0.5 * HEUN * (f0s[:, cols] + f) + kick
        xnb[:, cols] = xn.astype(BF16)
    resid = (obs_ref[...].astype(F32) - nn(xnb[...], c_ref[...])) * inv_ref[...]
    loglik = -0.5 * jnp.sum(resid * resid, axis=1, keepdims=True)

    peak = jnp.max(loglik, axis=0, keepdims=True)
    total = jnp.sum(jnp.exp(loglik - peak), axis=0, keepdims=True)
    norm_src[0] = jnp.where(iota((1, 128), 1) == 0, peak, total)
    exchange(2, norm_src, norm_tab, False)
    norm_tab[me] = norm_src[0]
    exchange_wait(2, norm_tab)
    table = norm_tab[...]
    peaks, totals = table[:, :, 0:1], table[:, :, 1:2]
    top = jnp.max(peaks, axis=0, keepdims=True)
    whole = jnp.sum(totals * jnp.exp(peaks - top), axis=0, keepdims=True)
    weight = jnp.exp(loglik - top[0]) / whole[0] * float(rows * devices)

    dmean = (weight * resid * inv_ref[...]).astype(BF16)
    for n in range(0, width, block):
        cols = slice(n, n + block)
        gxn = g_ref[:, cols].astype(F32) + nt(dmean, c_ref[cols, :])
        gxs[:, cols] = gxn
        gf[:rows, cols] = (0.5 * HEUN * gxn).astype(BF16)
    for n in range(0, hidden, block):
        cols = slice(n, n + block)
        one = nt(gf[:rows, :], w2_ref[cols, :]) * u1[:, cols]
        gp[:rows, cols] = one.astype(BF16)
        dots[:, cols] = jnp.sum(one, axis=0, keepdims=True)
    for n in range(0, width, block):
        cols = slice(n, n + block)
        gxn = gxs[:, cols]
        gxp = nt(gp[:rows, :], w1_ref[cols, :])
        both = gxn + gxp
        gf0 = 0.5 * HEUN * gxn + HEUN * gxp
        gf[rows:, cols] = gf0.astype(BF16)
        gxs[:, cols] = both
        d_b2 = jnp.sum(0.5 * HEUN * gxn + gf0, axis=0, keepdims=True)
        d_sigma = jnp.sum(both * noise_ref[:, cols].astype(F32), axis=0, keepdims=True)
        for j in range(block // 128):
            at = n // 128 + j
            accx[1, 1, at : at + 1, :] = d_b2[:, 128 * j : 128 * (j + 1)]
            accx[1, 2, at : at + 1, :] = d_sigma[:, 128 * j : 128 * (j + 1)]
    for n in range(0, hidden, block):
        cols = slice(n, n + block)
        zero = nt(gf[rows:, :], w2_ref[cols, :]) * u0[:, cols]
        gp[rows:, cols] = zero.astype(BF16)
        d_b1 = dots[:, cols] + jnp.sum(zero, axis=0, keepdims=True)
        for j in range(block // 128):
            at = n // 128 + j
            accx[1, 0, at : at + 1, :] = d_b1[:, 128 * j : 128 * (j + 1)]
    for n in range(0, width, block):
        cols = slice(n, n + block)
        gxs[:, cols] = gxs[:, cols] + nt(gp[rows:, :], w1_ref[cols, :])

    gx_high, gx_low = split(gxs[...])

    def give(i, carry):
        at = pl.multiple_of(i * group, group)
        onehot = jnp.where(iota((group * MOST, rows), 0) + at * MOST == flat, 1.0, 0.0).astype(BF16)
        out = nn(onehot, gx_high) + nn(onehot, gx_low)
        word, level = encode_wide(out.reshape(group, MOST, width))
        ret[pl.ds(at, group)] = jnp.concatenate([word, level], axis=1)
        return carry

    lax.fori_loop(0, devices // group, give, 0)
    exchange(3, ret, arr_ref, True)
    arr_ref[me] = ret[me]

    accx[1, 1, 4:8, :] = jnp.zeros((4, 128), F32)
    accx[1, 2, 4:8, :] = jnp.zeros((4, 128), F32)
    accx[1, pl.ds(3, chips - 3)] = jnp.zeros((chips - 3, 8, 128), F32)
    accx[0] = tn(xnb[...], dmean).reshape(chips, 8, 128)
    for n in range(0, hidden, block):
        acc2[n // 8 : (n + block) // 8] = tn(aa[:, n : n + block], gf[...]).reshape(block // 8, 8, width)
    for h in range(2):
        acc1[h * chips : (h + 1) * chips] = tn(xx[...], gp[:, h * width : (h + 1) * width]).reshape(chips, 8, width)

    swaps = []
    for i, (source, target) in enumerate(
        (
            (acc1.at[pl.ds((1 - core) * chips, chips)], in1),
            (acc2.at[pl.ds((1 - core) * chips, chips)], in2),
            (accx.at[1 - core], inx),
        )
    ):
        swap = pltpu.make_async_remote_copy(
            src_ref=source, dst_ref=target, send_sem=ssem.at[4 + i], recv_sem=rsem.at[4 + i],
            device_id=(other,), device_id_type=MESH,
        )
        swap.start()
        swaps.append(swap)
    for swap in swaps:
        swap.wait()

    step = 4

    def prepare(i, carry):
        at = pl.multiple_of(i * step, step)
        mine = pl.ds(at, step)
        held = pl.ds(core * chips + at, step)
        in1[mine] = in1[mine] + acc1[held]
        in2[mine] = in2[mine] + acc2[held]
        inx[mine] = inx[mine] + accx[core, mine]
        enc[mine] = encode_slice(in1[mine], in2[mine], inx[mine])
        return carry

    lax.fori_loop(0, chips // step, prepare, 0)

    def chips_send(stage, source, target):
        def send(k, carry):
            c = lax.rem(chip + k, chips)
            pltpu.make_async_remote_copy(
                src_ref=source(c), dst_ref=target, send_sem=ssem.at[stage], recv_sem=rsem.at[stage],
                device_id=(2 * c + core,), device_id_type=MESH,
            ).start()
            return carry

        lax.fori_loop(1, chips, send, 0)

    def chips_wait(stage, target):
        bytes_wait(target, ssem.at[stage])
        bytes_wait(target, rsem.at[stage])

    chips_send(7, lambda c: enc.at[c], got.at[chip])
    got[chip] = enc[chip]
    chips_wait(7, got.at[pl.ds(0, chips - 1)])

    def add(i, carry):
        one, two, rest = decode_slice(got[pl.ds(i, 1)])
        return carry[0] + one, carry[1] + two, carry[2] + rest

    zeros = (jnp.zeros((1, 8, width), F32), jnp.zeros((1, 8, width), F32), jnp.zeros((1, 8, 128), F32))
    sums = lax.fori_loop(0, chips, add, zeros)
    fin[...] = encode_slice(*sums)

    chips_send(8, lambda c: fin.at[0], all_ref.at[core, chip])
    all_ref[core, chip] = fin[0]
    chips_wait(8, all_ref.at[0, pl.ds(0, chips - 1)])

    last = pltpu.make_async_remote_copy(
        src_ref=all_ref.at[core], dst_ref=all_ref.at[core], send_sem=ssem.at[9], recv_sem=rsem.at[9],
        device_id=(other,), device_id_type=MESH,
    )
    last.start()
    last.wait()
    exchange_wait(3, arr_ref)


def finish_kernel(inc_ref, arr_ref, all_ref, dprev_ref, dw1_ref, dw2_ref, dc_ref, db1_ref, db2_ref, dsigma_ref):
    devices = inc_ref.shape[0]
    chips = devices // 2
    rows, width = dprev_ref.shape
    group = 16

    def place(i, carry):
        at = pl.multiple_of(i * group, group)
        column = wanted_columns(inc_ref[pl.ds(at, group)])
        onehot = jnp.where(column == iota((group, MOST, rows), 2).astype(F32), 1.0, 0.0)
        onehot = onehot.reshape(group * MOST, rows).astype(BF16)
        word = arr_ref[pl.ds(at, group)]
        value = decode_wide(word[:, :16], word[:, 16:17]).reshape(group * MOST, width)
        high, low = split(value)
        return carry + tn(onehot, high) + tn(onehot, low)

    dprev_ref[...] = lax.fori_loop(0, devices // group, place, jnp.zeros((rows, width), F32))

    step = 4
    for core in range(2):

        def spread(i, carry):
            at = pl.multiple_of(i * step, step)
            one, two, rest = decode_slice(all_ref[core, pl.ds(at, step)])
            lines = pl.ds(pl.multiple_of(at * 8, step * 8), step * 8)
            dw1_ref[lines, core * width : (core + 1) * width] = one.reshape(step * 8, width)
            far = pl.ds(pl.multiple_of(at * 8 + core * chips * 8, step * 8), step * 8)
            dw2_ref[far, :] = two.reshape(step * 8, width)
            if core == 0:
                dc_ref[lines, :] = rest.reshape(step * 8, 128)
            return carry

        lax.fori_loop(0, chips // step, spread, 0)
    _, _, small = decode_slice(all_ref[1, 0:3])
    db1_ref[...] = small[0]
    db2_ref[...] = small[1, :4]
    dsigma_ref[...] = small[2, :4]


def per_device(x_prev, anc_owner, anc_row, noise, g_new, obs, w1, b1, w2, b2, c_obs, inv_scale, sigma):
    devices = lax.axis_size("particle")
    chips = devices // 2
    rows, width = x_prev.shape
    hidden = w1.shape[1]
    vmem = pl.BlockSpec(memory_space=pltpu.VMEM)
    inc, arr, whole = pl.pallas_call(
        functools.partial(main_kernel, devices),
        out_shape=(
            jax.ShapeDtypeStruct((devices, 1, 128), F32),
            jax.ShapeDtypeStruct((devices, 17, 128), I32),
            jax.ShapeDtypeStruct((2, chips, 40, 128), I32),
        ),
        in_specs=[vmem] * 13,
        out_specs=(vmem, vmem, vmem),
        scratch_shapes=[
            pltpu.VMEM((devices, 1, 128), F32),
            pltpu.VMEM((devices, 128), F32),
            pltpu.VMEM((devices, 2 * MOST, width // 2), BF16),
            pltpu.VMEM((devices, 2 * MOST, width // 2), BF16),
            pltpu.VMEM((1, 1, 128), F32),
            pltpu.VMEM((devices, 1, 128), F32),
            pltpu.VMEM((devices, 17, 128), I32),
            pltpu.VMEM((2 * rows, width), BF16),
            pltpu.VMEM((2 * rows, hidden), BF16),
            pltpu.VMEM((2 * rows, width), BF16),
            pltpu.VMEM((2 * rows, hidden), BF16),
            pltpu.VMEM((rows, hidden), F32),
            pltpu.VMEM((rows, hidden), F32),
            pltpu.VMEM((rows, width), BF16),
            pltpu.VMEM((rows, width), F32),
            pltpu.VMEM((rows, width), F32),
            pltpu.VMEM((1, hidden), F32),
            pltpu.VMEM((devices, 8, width), F32),
            pltpu.VMEM((devices, 8, width), F32),
            pltpu.VMEM((2, chips, 8, 128), F32),
            pltpu.VMEM((chips, 8, width), F32),
            pltpu.VMEM((chips, 8, width), F32),
            pltpu.VMEM((chips, 8, 128), F32),
            pltpu.VMEM((chips, 40, 128), I32),
            pltpu.VMEM((chips, 40, 128), I32),
            pltpu.VMEM((1, 40, 128), I32),
            pltpu.SemaphoreType.DMA((10,)),
            pltpu.SemaphoreType.DMA((10,)),
        ],
        compiler_params=pltpu.CompilerParams(collective_id=0, has_side_effects=True, vmem_limit_bytes=56 * 2**20),
        name="heun_step",
    )(
        x_prev, anc_owner.reshape(1, rows), anc_row.reshape(1, rows), noise, g_new, obs,
        w1, b1.reshape(1, hidden), w2, b2.reshape(1, width), c_obs, inv_scale.reshape(1, -1), sigma.reshape(1, width),
    )
    d_prev, d_w1, d_w2, d_c, d_b1, d_b2, d_sigma = pl.pallas_call(
        finish_kernel,
        out_shape=(
            jax.ShapeDtypeStruct((rows, width), F32),
            jax.ShapeDtypeStruct((width, hidden), F32),
            jax.ShapeDtypeStruct((hidden, width), F32),
            jax.ShapeDtypeStruct((width, 128), F32),
            jax.ShapeDtypeStruct((hidden // 128, 128), F32),
            jax.ShapeDtypeStruct((width // 128, 128), F32),
            jax.ShapeDtypeStruct((width // 128, 128), F32),
        ),
        in_specs=[vmem] * 3,
        out_specs=(vmem,) * 7,
        compiler_params=pltpu.CompilerParams(vmem_limit_bytes=40 * 2**20),
        name="place_results",
    )(inc, arr, whole)
    return (d_prev, d_w1, d_b1.reshape(hidden), d_w2, d_b2.reshape(width), d_c, d_sigma.reshape(width))


def solution(mesh):
    split_rows = P("particle", None)
    return jax.shard_map(
        per_device,
        mesh=mesh,
        in_specs=(split_rows, split_rows, P("particle"), split_rows, split_rows, split_rows) + (P(),) * 7,
        out_specs=(split_rows, P(), P(), P(), P(), P(), P()),
        check_vma=False,
    )
```

time: 399 us -> 128 us (0.32)
  blocking collectives: 231 us -> 0 us
  Pallas kernels: 0 us -> 123 us
  waiting for transfers between devices: 84.5 us -> 0 us
  local copies, waits for them, and re-layouts: 24.6 us -> 3.98 us
  matrix products: 19.7 us -> 0 us
  between operations: 14.4 us -> 0.66 us
  other arithmetic: 13.7 us -> 0 us
  starting transfers between devices: 9.63 us -> 0 us
    psum x2 -> x0, blocking collectives: 148 us -> none  [the longest x1 85 us: sum_grads(): lax.psum((grads[0], grads[1], grads[2], grads[3], grads[4], grads[5]), 'p...]
    pallas_call x0 -> x2, Pallas kernels: none -> 123 us  [the longest x1 115 us: per_device(): pl.pallas_call(functools.partial(main_kernel, devices), out_shape=(jax.Sh...]
    psum x1 -> x0, waiting for transfers between devices: 66 us -> none  [sum_grads(): lax.psum((grads[0], grads[1], grads[2], grads[3], grads[4], grads[5]), 'p...]
    pmax x1 -> x0, blocking collectives: 62.5 us -> none  [normalize(): peak = lax.pmax(local_peak, 'particle')]
    all_to_all x1 -> x0, blocking collectives: 20.8 us -> none  [per_device(): lax.all_to_all(wanted, 'particle', split_axis=0, concat_axis=0, tiled=True)]
    dot_general x15 -> x0, matrix products: 19.7 us -> none  [the longest x5 8.25 us: rdot(): lax.dot_general(left, right, (((1,), (1,)), ((), ())), preferred_element_...]
    all_to_all x2 -> x0, waiting for transfers between devices: 18.5 us -> none  [the longest x1 18.5 us: per_device(): lax.all_to_all(sent_rows, 'particle', split_axis=0, concat_axis=0, tiled=...]
    all_to_all x2 -> x0, starting transfers between devices: 9.59 us -> none  [the longest x1 4.98 us: per_device(): lax.all_to_all(returned, 'particle', split_axis=0, concat_axis=0, tiled=T...]
  transfers between devices with their start and end apart: 3 -> 0, of which waited for: 2 -> 0; matrix products, arithmetic and copies ran while one was open for 4% -> 0% of each run, Pallas kernels for 0% -> 0%
where the time goes in v1:
time: 128 us
  Pallas kernels  123 us (96%)
  local copies, waits for them, and re-layouts  3.98 us (3%)
    pallas_call x1, Pallas kernels, per_device(): pl.pallas_call(functools.partial(main_kernel, devices), out_shape=(jax.Sh...  115 us
    pallas_call x1, Pallas kernels, per_device(): pl.pallas_call(finish_kernel, out_shape=(jax.ShapeDtypeStruct((rows, widt...  8.73 us
    unnamed x6, local copies, waits for them, and re-layouts  3.98 us

profile of v1, /device:TPU:1, one launch (start us, length us, event | category | flops | bytes accessed | tf_op | source)
XLA Modules:
  0.0 127.9 jit_solution(6603107540286567658)
XLA Ops:
  0.6 114.6 %heun_step.1 = (f32[128,1,128]{2,1,0:T(1,128)}, s32[128,17,128]{2,1,0:T(8,128)}, s32[2,64,40,128]{3,2,1,0:T(8,128)}) custom-call(bf16[512,512]{1,0:T(8,128)(2,1)} %x_ref.1, s32[1,512]{1,0:T(1,128)} %bitcast.10, s32[1,512]{1,0:T(1,128)} %bitcast.11, bf16[512,512]{1,0:T(8,128)(2,1)} %noise_ref.1, bf16[512,512]{1,0:T(8,128)(2,1)} %g_ref.1, ...), custom_call_target="tpu_custom_call" | custom-call | tf_op jit(solution)/shard_map/heun_step/pallas_call | solution.py:423
  115.2 0.0 copy-start
  115.2 1.7 %copy-done = s32[2,64,40,128]{3,2,1,0:T(8,128)S(1)} copy-done((s32[2,64,40,128]{3,2,1,0:T(8,128)S(1)}, s32[2,64,40,128]{3,2,1,0:T(8,128)}, u32[]{:S(2)}) %copy-start) | copy-done | bytes 2621464
  117.0 0.0 copy-start.1
  117.0 1.4 %copy-done.1 = s32[128,17,128]{2,1,0:T(8,128)S(1)} copy-done((s32[128,17,128]{2,1,0:T(8,128)S(1)}, s32[128,17,128]{2,1,0:T(8,128)}, u32[]{:S(2)}) %copy-start.1) | copy-done | bytes 1114136
  118.4 0.0 copy-start.2
  118.4 0.8 copy-done.2
  119.2 8.7 %place_results.1 = (f32[512,512]{1,0:T(8,128)}, f32[512,1024]{1,0:T(8,128)}, f32[1024,512]{1,0:T(8,128)}, f32[512,128]{1,0:T(8,128)}, f32[8,128]{1,0:T(8,128)}, /*index=5*/f32[4,128]{1,0:T(4,128)}, f32[4,128]{1,0:T(4,128)}) custom-call(f32[128,1,128]{2,1,0:T(1,128)S(1)} %copy-done.2, s32[128,17,128]{2,1,0:T(8,128)S(1)} %copy-done.1, ...), custom_call_target="tpu_custom_call" | custom-call | tf_op jit(solution)/shard_map/place_results/pallas_call | solution.py:468
Async XLA Ops:
  115.2 1.7 %copy-start = (s32[2,64,40,128]{3,2,1,0:T(8,128)S(1)}, s32[2,64,40,128]{3,2,1,0:T(8,128)}, u32[]{:S(2)}) copy-start(s32[2,64,40,128]{3,2,1,0:T(8,128)} %get-tuple-element.19.all_ref) | copy-start | bytes 7864324
  117.0 1.4 %copy-start.1 = (s32[128,17,128]{2,1,0:T(8,128)S(1)}, s32[128,17,128]{2,1,0:T(8,128)}, u32[]{:S(2)}) copy-start(s32[128,17,128]{2,1,0:T(8,128)} %get-tuple-element.18.arr_ref) | copy-start | bytes 3342340
  118.4 0.8 copy-start.2

commit v2 on v1

--- a/solution.py
+++ b/solution.py
@@ -12,6 +12,7 @@
 F32 = jnp.float32
 BF16 = jnp.bfloat16
 I32 = jnp.int32
+HOP, BACK = 11, 35
 MOST = 8
 LOGSTEP = 65536.0
 TOP = 32767.0
@@ -72,20 +73,23 @@
     return jnp.concatenate([low0 * scale, low1 * scale, high0 * scale, high1 * scale], axis=2)
 
 
-def encode_slice(one, two, rest):
-    word1, level1 = encode_wide(one)
-    word2, level2 = encode_wide(two)
-    code3, level3 = encode(rest)
-    word3 = pack(code3[:, :4], code3[:, 4:])
-    return jnp.concatenate([word1, word2, word3, level1, level2, level3, level3], axis=1)
+def encode_slice(value):
+    codes, levels = zip(*(encode(value[:, :, 128 * b : 128 * (b + 1)]) for b in range(3)))
+    lane = iota((value.shape[0], 1, 128), 2)
+    level = jnp.where(lane == 0, levels[0], jnp.where(lane == 1, levels[1], levels[2]))
+    return jnp.concatenate([pack(codes[0], codes[1]), pack(codes[2][:, :4], codes[2][:, 4:]), level], axis=1)
 
 
 def decode_slice(word):
-    one = decode_wide(word[:, 0:16], word[:, 36:37])
-    two = decode_wide(word[:, 16:32], word[:, 37:38])
-    scale = unscale(word[:, 38:39])
-    low, high = unpack(word[:, 32:36])
-    return one, two, jnp.concatenate([low * scale, high * scale], axis=1)
+    scale = unscale(word[:, 12:13])
+    low, high = unpack(word[:, :8])
+    top, bottom = unpack(word[:, 8:12])
+    last = jnp.concatenate([top, bottom], axis=1)
+    return low * scale[:, :, 0:1], high * scale[:, :, 1:2], last * scale[:, :, 2:3]
+
+
+def joined(blocks):
+    return jnp.concatenate(blocks, axis=2)
 
 
 def wanted_columns(table):
@@ -102,18 +106,22 @@
 
 def main_kernel(
     devices,
-    x_ref, owner_ref, row_ref, noise_ref, g_ref, obs_ref, w1_ref, b1_ref, w2_ref, b2_ref, c_ref, inv_ref, sigma_ref,
-    inc_ref, arr_ref, all_ref,
+    x_hbm, owner_ref, row_ref, noise_hbm, g_hbm, obs_hbm, w1_hbm, b1_ref, w2_hbm, b2_ref, c_hbm, inv_ref, sigma_ref,
+    dprev_hbm, all_hbm,
+    x_ref, noise_ref, g_ref, obs_ref, w1_ref, w2_ref, c_ref, dprev, inc_ref, arr_ref,
     wtab, wrow, send_rows, recv_rows, norm_src, norm_tab, ret, xx, aa, gf, gp, u0, u1, xnb, f0s, gxs, dots,
-    acc1, acc2, accx, in1, in2, inx, enc, got, fin,
-    ssem, rsem,
+    acc1, acc2, accx, in1, in2, inx, sums, enc1, got1, half, enc2, got2, fin, whole,
+    ssem, rsem, lsem, s1, r1, s2, r2, s3, r3, s4, r4, s5, r5, out_sem,
 ):
     me = lax.axis_index("particle")
     rows, width = x_ref.shape
     hidden = w1_ref.shape[1]
     chips = devices // 2
-    chip, core = lax.div(me, 2), lax.rem(me, 2)
+    core = lax.rem(me, 2)
     other = me + 1 - 2 * core
+    stride = {"x": 2, "z": 8, "y": 32}
+    coordinate = {axis: lax.rem(lax.div(me, by), 4) for axis, by in stride.items()}
+    streams = (("x", "y", "z"), ("z", "x", "y"), ("y", "z", "x"))
 
     barrier = pltpu.get_barrier_semaphore()
 
@@ -122,6 +130,22 @@
         return carry
 
     lax.fori_loop(1, devices, greet, 0)
+    loads = [
+        pltpu.make_async_copy(source, target, lsem.at[i])
+        for i, (source, target) in enumerate(
+            (
+                (x_hbm, x_ref),
+                (w1_hbm, w1_ref),
+                (w2_hbm, w2_ref),
+                (noise_hbm, noise_ref),
+                (g_hbm, g_ref),
+                (obs_hbm, obs_ref),
+                (c_hbm, c_ref),
+            )
+        )
+    ]
+    for load in loads:
+        load.start()
 
     owner = owner_ref[...]
     row = row_ref[...]
@@ -142,21 +166,22 @@
 
     lax.fori_loop(0, devices, spread, 0, unroll=8)
     eye = jnp.where(iota((rows, rows), 0) == iota((rows, rows), 1), 1.0, 0.0).astype(BF16)
-    pair = jnp.where(part == 0, owner.astype(F32), jnp.where(part == 1, slot, 0.0)).astype(BF16)
+    turn = jnp.bitwise_and((me - owner + devices) * BACK, devices - 1)
+    pair = jnp.where(part == 0, turn.astype(F32), jnp.where(part == 1, slot, 0.0)).astype(BF16)
     turned = nt(eye, pair)
     place = turned[:, 0:1] * (2 * MOST) + turned[:, 1:2]
     flat = owner * MOST + slot.astype(I32)
 
     pl.semaphore_wait(barrier, devices - 1)
 
-    def exchange(stage, source, target, partner_block):
+    def exchange(stage, source, target, per_partner, by_turn=False):
         def send(k, carry):
-            d = lax.rem(me + k, devices)
+            d = lax.rem(me + lax.rem(HOP * k, devices), devices)
             pltpu.make_async_remote_copy(
-                src_ref=source.at[d] if partner_block else source.at[0],
-                dst_ref=target.at[me],
+                src_ref=source.at[d] if per_partner else source.at[0],
+                dst_ref=target.at[k] if by_turn else target.at[me],
                 send_sem=ssem.at[stage],
-                recv_sem=rsem.at[stage],
+                recv_sem=rsem.at[4 + lax.div(k, devices // 4)] if by_turn else rsem.at[stage],
                 device_id=(d,),
                 device_id_type=MESH,
             ).start()
@@ -187,24 +212,28 @@
         send_rows[pl.ds(at, group)] = halves.astype(BF16)
         return carry
 
+    loads[0].wait()
     lax.fori_loop(0, devices // group, gather, 0)
-    exchange(1, send_rows, recv_rows, True)
-    recv_rows[me] = send_rows[me]
-    exchange_wait(1, recv_rows)
-
-    def start(i, carry):
-        left, right = carry
-        at = pl.multiple_of(i * group, group)
-        block = recv_rows[pl.ds(at, group)].reshape(group * 2 * MOST, width // 2)
-        index = (iota((rows, group * 2 * MOST), 1) + at * (2 * MOST)).astype(F32)
+    exchange(1, send_rows, recv_rows, True, by_turn=True)
+    recv_rows[0] = send_rows[me]
+    for load in loads[1:]:
+        load.wait()
+
+    left = jnp.zeros((rows, width // 2), F32)
+    right = left
+    quarter = devices // 4
+    for i in range(4):
+        first = 1 if i == 0 else 0
+        bytes_wait(recv_rows.at[pl.ds(0, quarter - first)], rsem.at[4 + i])
+        block = recv_rows[i * quarter : (i + 1) * quarter].reshape(quarter * 2 * MOST, width // 2)
+        index = (iota((rows, quarter * 2 * MOST), 1) + i * quarter * 2 * MOST).astype(F32)
         take_left = jnp.where(place == index, 1.0, 0.0).astype(BF16)
         take_right = jnp.where(place + MOST == index, 1.0, 0.0).astype(BF16)
-        return left + nn(take_left, block), right + nn(take_right, block)
-
-    none = jnp.zeros((rows, width // 2), F32)
-    left, right = lax.fori_loop(0, devices // group, start, (none, none))
+        left = left + nn(take_left, block)
+        right = right + nn(take_right, block)
     xx[rows:, : width // 2] = left.astype(BF16)
     xx[rows:, width // 2 :] = right.astype(BF16)
+    bytes_wait(recv_rows.at[pl.ds(0, devices - 1)], ssem.at[1])
 
     x0 = xx[rows:, :]
     block = 256
@@ -241,8 +270,8 @@
     table = norm_tab[...]
     peaks, totals = table[:, :, 0:1], table[:, :, 1:2]
     top = jnp.max(peaks, axis=0, keepdims=True)
-    whole = jnp.sum(totals * jnp.exp(peaks - top), axis=0, keepdims=True)
-    weight = jnp.exp(loglik - top[0]) / whole[0] * float(rows * devices)
+    mass = jnp.sum(totals * jnp.exp(peaks - top), axis=0, keepdims=True)
+    weight = jnp.exp(loglik - top[0]) / mass[0] * float(rows * devices)
 
     dmean = (weight * resid * inv_ref[...]).astype(BF16)
     for n in range(0, width, block):
@@ -301,23 +330,20 @@
     accx[0] = tn(xnb[...], dmean).reshape(chips, 8, 128)
     for n in range(0, hidden, block):
         acc2[n // 8 : (n + block) // 8] = tn(aa[:, n : n + block], gf[...]).reshape(block // 8, 8, width)
-    for h in range(2):
-        acc1[h * chips : (h + 1) * chips] = tn(xx[...], gp[:, h * width : (h + 1) * width]).reshape(chips, 8, width)
-
-    swaps = []
-    for i, (source, target) in enumerate(
-        (
-            (acc1.at[pl.ds((1 - core) * chips, chips)], in1),
-            (acc2.at[pl.ds((1 - core) * chips, chips)], in2),
-            (accx.at[1 - core], inx),
-        )
-    ):
+
+    def core_swap(i, source, target):
         swap = pltpu.make_async_remote_copy(
-            src_ref=source, dst_ref=target, send_sem=ssem.at[4 + i], recv_sem=rsem.at[4 + i],
+            src_ref=source, dst_ref=target, send_sem=ssem.at[8 + i], recv_sem=rsem.at[8 + i],
             device_id=(other,), device_id_type=MESH,
         )
         swap.start()
-        swaps.append(swap)
+        return swap
+
+    theirs = pl.ds((1 - core) * chips, chips)
+    swaps = [core_swap(0, acc2.at[theirs], in2), core_swap(1, accx.at[1 - core], inx)]
+    for h in range(2):
+        acc1[h * chips : (h + 1) * chips] = tn(xx[...], gp[:, h * width : (h + 1) * width]).reshape(chips, 8, width)
+    swaps.append(core_swap(2, acc1.at[theirs], in1))
     for swap in swaps:
         swap.wait()
 
@@ -327,109 +353,184 @@
         at = pl.multiple_of(i * step, step)
         mine = pl.ds(at, step)
         held = pl.ds(core * chips + at, step)
-        in1[mine] = in1[mine] + acc1[held]
-        in2[mine] = in2[mine] + acc2[held]
-        inx[mine] = inx[mine] + accx[core, mine]
-        enc[mine] = encode_slice(in1[mine], in2[mine], inx[mine])
+        one = in1[mine] + acc1[held]
+        two = in2[mine] + acc2[held]
+        rest = inx[mine] + accx[core, mine]
+        values = (one[:, :, :384], two[:, :, :384], joined([one[:, :, 384:], two[:, :, 384:], rest]))
+        for t in range(3):
+            sums[t, mine] = values[t]
+            enc1[t, mine] = encode_slice(values[t])
         return carry
 
     lax.fori_loop(0, chips // step, prepare, 0)
 
-    def chips_send(stage, source, target):
-        def send(k, carry):
-            c = lax.rem(chip + k, chips)
-            pltpu.make_async_remote_copy(
-                src_ref=source(c), dst_ref=target, send_sem=ssem.at[stage], recv_sem=rsem.at[stage],
-                device_id=(2 * c + core,), device_id_type=MESH,
-            ).start()
-            return carry
-
-        lax.fori_loop(1, chips, send, 0)
-
-    def chips_wait(stage, target):
-        bytes_wait(target, ssem.at[stage])
-        bytes_wait(target, rsem.at[stage])
-
-    chips_send(7, lambda c: enc.at[c], got.at[chip])
-    got[chip] = enc[chip]
-    chips_wait(7, got.at[pl.ds(0, chips - 1)])
-
-    def add(i, carry):
-        one, two, rest = decode_slice(got[pl.ds(i, 1)])
-        return carry[0] + one, carry[1] + two, carry[2] + rest
-
-    zeros = (jnp.zeros((1, 8, width), F32), jnp.zeros((1, 8, width), F32), jnp.zeros((1, 8, 128), F32))
-    sums = lax.fori_loop(0, chips, add, zeros)
-    fin[...] = encode_slice(*sums)
-
-    chips_send(8, lambda c: fin.at[0], all_ref.at[core, chip])
-    all_ref[core, chip] = fin[0]
-    chips_wait(8, all_ref.at[0, pl.ds(0, chips - 1)])
-
-    last = pltpu.make_async_remote_copy(
-        src_ref=all_ref.at[core], dst_ref=all_ref.at[core], send_sem=ssem.at[9], recv_sem=rsem.at[9],
-        device_id=(other,), device_id_type=MESH,
-    )
-    last.start()
-    last.wait()
+    plane = chips // 4
+    along = []
+    for k in (2, 1, 3):
+        for t, (axis, _, _) in enumerate(streams):
+            there = lax.rem(coordinate[axis] + k, 4)
+            copy = pltpu.make_async_remote_copy(
+                src_ref=enc1.at[t, pl.ds(there * plane, plane)], dst_ref=got1.at[t, k - 1],
+                send_sem=s1.at[3 * t + k - 1], recv_sem=r1.at[3 * t + k - 1],
+                device_id=(me + (there - coordinate[axis]) * stride[axis],), device_id_type=MESH,
+            )
+            copy.start()
+            along.append(copy)
+
     exchange_wait(3, arr_ref)
 
-
-def finish_kernel(inc_ref, arr_ref, all_ref, dprev_ref, dw1_ref, dw2_ref, dc_ref, db1_ref, db2_ref, dsigma_ref):
-    devices = inc_ref.shape[0]
-    chips = devices // 2
-    rows, width = dprev_ref.shape
-    group = 16
-
-    def place(i, carry):
+    def settle(i, carry):
         at = pl.multiple_of(i * group, group)
         column = wanted_columns(inc_ref[pl.ds(at, group)])
         onehot = jnp.where(column == iota((group, MOST, rows), 2).astype(F32), 1.0, 0.0)
         onehot = onehot.reshape(group * MOST, rows).astype(BF16)
         word = arr_ref[pl.ds(at, group)]
         value = decode_wide(word[:, :16], word[:, 16:17]).reshape(group * MOST, width)
-        high, low = split(value)
-        return carry + tn(onehot, high) + tn(onehot, low)
-
-    dprev_ref[...] = lax.fori_loop(0, devices // group, place, jnp.zeros((rows, width), F32))
-
-    step = 4
+        upper, lower = split(value)
+        return carry + tn(onehot, upper) + tn(onehot, lower)
+
+    dprev[...] = lax.fori_loop(0, devices // group, settle, jnp.zeros((rows, width), F32))
+    settled = pltpu.make_async_copy(dprev, dprev_hbm, lsem.at[7])
+    settled.start()
+
+    for copy in along:
+        copy.wait()
+    home = [coordinate[axis] * plane for axis, _, _ in streams]
+    spot = [coordinate[u] * 4 + coordinate[v] for _, u, v in streams]
+    for t in range(3):
+
+        def fold(i, carry):
+            at = pl.multiple_of(i * step, step)
+            value = sums[t, pl.ds(home[t] + at, step)]
+            for k in range(3):
+                value = value + joined(decode_slice(got1[t, k, pl.ds(at, step)]))
+            half[t, pl.ds(at, step)] = value
+            enc2[t, pl.ds(at, step)] = encode_slice(value)
+            return carry
+
+        lax.fori_loop(0, plane // step, fold, 0)
+
+    def over_plane(t, source, target, send_sem, recv_sem):
+        axis, u, v = streams[t]
+        base = core + coordinate[axis] * stride[axis]
+
+        def send(k, carry):
+            there = lax.rem(spot[t] + k, plane)
+            d = base + lax.div(there, 4) * stride[u] + lax.rem(there, 4) * stride[v]
+            pltpu.make_async_remote_copy(
+                src_ref=source(there), dst_ref=target(k), send_sem=send_sem, recv_sem=recv_sem,
+                device_id=(d,), device_id_type=MESH,
+            ).start()
+            return carry
+
+        lax.fori_loop(1, plane, send, 0)
+
+    for t in range(3):
+        over_plane(t, lambda there: enc2.at[t, there], lambda k: got2.at[t, k - 1], s2.at[t], r2.at[t])
+    for t in range(3):
+        bytes_wait(got2.at[t], r2.at[t])
+        value = half[t, spot[t]][None]
+        for k in range(0, plane - 1, 5):
+            value = value + jnp.sum(joined(decode_slice(got2[t, k : k + 5])), axis=0, keepdims=True)
+        fin[t] = encode_slice(value)
+        whole[t, home[t] + spot[t]] = fin[t, 0]
+        over_plane(t, lambda there: fin.at[t, 0], lambda k: whole.at[t, home[t] + spot[t]], s3.at[t], r3.at[t])
+
+    outs = []
+
+    def publish(i, t, first):
+        source = whole.at[t, pl.ds(first, plane)]
+        target = all_hbm.at[core, t, pl.ds(first, plane)]
+        keep = pltpu.make_async_copy(source, target, out_sem.at[i])
+        give = pltpu.make_async_remote_copy(
+            src_ref=source, dst_ref=target, send_sem=s5.at[i], recv_sem=r5.at[i],
+            device_id=(other,), device_id_type=MESH,
+        )
+        keep.start()
+        give.start()
+        outs.append(keep)
+        outs.append(give)
+
+    along = []
+    for t, (axis, _, _) in enumerate(streams):
+        bytes_wait(got2.at[t], r3.at[t])
+        for k in (2, 1, 3):
+            there = lax.rem(coordinate[axis] + k, 4)
+            held = whole.at[t, pl.ds(home[t], plane)]
+            copy = pltpu.make_async_remote_copy(
+                src_ref=held, dst_ref=held, send_sem=s4.at[3 * t + k - 1], recv_sem=r4.at[3 * t + k - 1],
+                device_id=(me + (there - coordinate[axis]) * stride[axis],), device_id_type=MESH,
+            )
+            copy.start()
+            along.append((t, k, copy))
+        publish(t, t, home[t])
+    for t, k, copy in along:
+        copy.wait_recv()
+        first = lax.rem(coordinate[streams[t][0]] + 4 - k, 4) * plane
+        publish(3 + 3 * t + k - 1, t, first)
+    for t, k, copy in along:
+        copy.wait_send()
+    for t in range(3):
+        bytes_wait(got2.at[t], s2.at[t])
+        bytes_wait(got2.at[t], s3.at[t])
+    for copy in outs:
+        copy.wait()
+    settled.wait()
+
+
+def finish_kernel(dp_ref, all_ref, dprev_ref, dw1_ref, dw2_ref, dc_ref, db1_ref, db2_ref, dsigma_ref):
+    i = pl.program_id(0)
+    step = all_ref.shape[2]
+    width = dprev_ref.shape[1]
+    dprev_ref[...] = dp_ref[...]
     for core in range(2):
-
-        def spread(i, carry):
-            at = pl.multiple_of(i * step, step)
-            one, two, rest = decode_slice(all_ref[core, pl.ds(at, step)])
-            lines = pl.ds(pl.multiple_of(at * 8, step * 8), step * 8)
-            dw1_ref[lines, core * width : (core + 1) * width] = one.reshape(step * 8, width)
-            far = pl.ds(pl.multiple_of(at * 8 + core * chips * 8, step * 8), step * 8)
-            dw2_ref[far, :] = two.reshape(step * 8, width)
-            if core == 0:
-                dc_ref[lines, :] = rest.reshape(step * 8, 128)
-            return carry
-
-        lax.fori_loop(0, chips // step, spread, 0)
-    _, _, small = decode_slice(all_ref[1, 0:3])
-    db1_ref[...] = small[0]
-    db2_ref[...] = small[1, :4]
-    dsigma_ref[...] = small[2, :4]
+        first, second, third = (decode_slice(all_ref[core, t]) for t in range(3))
+        for b in range(4):
+            one = first[b] if b < 3 else third[0]
+            two = second[b] if b < 3 else third[1]
+            at = core * width + 128 * b
+            dw1_ref[:, at : at + 128] = one.reshape(step * 8, 128)
+            dw2_ref[core, :, 128 * b : 128 * (b + 1)] = two.reshape(step * 8, 128)
+        rest = third[2]
+        if core == 0:
+            dc_ref[...] = rest.reshape(step * 8, 128)
+        else:
+
+            @pl.when(i == 0)
+            def _():
+                db1_ref[...] = rest[0]
+                db2_ref[...] = rest[1, :4]
+                dsigma_ref[...] = rest[2, :4]
 
 
 def per_device(x_prev, anc_owner, anc_row, noise, g_new, obs, w1, b1, w2, b2, c_obs, inv_scale, sigma):
     devices = lax.axis_size("particle")
     chips = devices // 2
+    plane = chips // 4
     rows, width = x_prev.shape
     hidden = w1.shape[1]
     vmem = pl.BlockSpec(memory_space=pltpu.VMEM)
-    inc, arr, whole = pl.pallas_call(
+    anywhere = pl.BlockSpec(memory_space=pl.ANY)
+    dma = pltpu.SemaphoreType.DMA
+    d_prev, sums = pl.pallas_call(
         functools.partial(main_kernel, devices),
         out_shape=(
-            jax.ShapeDtypeStruct((devices, 1, 128), F32),
-            jax.ShapeDtypeStruct((devices, 17, 128), I32),
-            jax.ShapeDtypeStruct((2, chips, 40, 128), I32),
+            jax.ShapeDtypeStruct((rows, width), F32),
+            jax.ShapeDtypeStruct((2, 3, chips, 13, 128), I32),
         ),
-        in_specs=[vmem] * 13,
-        out_specs=(vmem, vmem, vmem),
+        in_specs=[anywhere, vmem, vmem, anywhere, anywhere, anywhere, anywhere, vmem, anywhere, vmem, anywhere, vmem, vmem],
+        out_specs=(anywhere, anywhere),
         scratch_shapes=[
+            pltpu.VMEM((rows, width), BF16),
+            pltpu.VMEM((rows, width), BF16),
+            pltpu.VMEM((rows, width), BF16),
+            pltpu.VMEM((rows, 128), BF16),
+            pltpu.VMEM((width, hidden), BF16),
+            pltpu.VMEM((hidden, width), BF16),
+            pltpu.VMEM((width, 128), BF16),
+            pltpu.VMEM((rows, width), F32),
+            pltpu.VMEM((devices, 1, 128), F32),
+            pltpu.VMEM((devices, 17, 128), I32),
             pltpu.VMEM((devices, 1, 128), F32),
             pltpu.VMEM((devices, 128), F32),
             pltpu.VMEM((devices, 2 * MOST, width // 2), BF16),
@@ -453,35 +554,57 @@
             pltpu.VMEM((chips, 8, width), F32),
             pltpu.VMEM((chips, 8, width), F32),
             pltpu.VMEM((chips, 8, 128), F32),
-            pltpu.VMEM((chips, 40, 128), I32),
-            pltpu.VMEM((chips, 40, 128), I32),
-            pltpu.VMEM((1, 40, 128), I32),
-            pltpu.SemaphoreType.DMA((10,)),
-            pltpu.SemaphoreType.DMA((10,)),
+            pltpu.VMEM((3, chips, 8, 384), F32),
+            pltpu.VMEM((3, chips, 13, 128), I32),
+            pltpu.VMEM((3, 3, plane, 13, 128), I32),
+            pltpu.VMEM((3, plane, 8, 384), F32),
+            pltpu.VMEM((3, plane, 13, 128), I32),
+            pltpu.VMEM((3, plane - 1, 13, 128), I32),
+            pltpu.VMEM((3, 1, 13, 128), I32),
+            pltpu.VMEM((3, chips, 13, 128), I32),
+            dma((12,)), dma((12,)), dma((8,)),
+            dma((9,)), dma((9,)), dma((3,)), dma((3,)), dma((3,)), dma((3,)), dma((9,)), dma((9,)),
+            dma((12,)), dma((12,)), dma((12,)),
         ],
-        compiler_params=pltpu.CompilerParams(collective_id=0, has_side_effects=True, vmem_limit_bytes=56 * 2**20),
+        compiler_params=pltpu.CompilerParams(collective_id=0, has_side_effects=True, vmem_limit_bytes=58 * 2**20),
         name="heun_step",
     )(
         x_prev, anc_owner.reshape(1, rows), anc_row.reshape(1, rows), noise, g_new, obs,
         w1, b1.reshape(1, hidden), w2, b2.reshape(1, width), c_obs, inv_scale.reshape(1, -1), sigma.reshape(1, width),
     )
+    step = 8
+    lines = step * 8
     d_prev, d_w1, d_w2, d_c, d_b1, d_b2, d_sigma = pl.pallas_call(
         finish_kernel,
+        grid=(chips // step,),
         out_shape=(
             jax.ShapeDtypeStruct((rows, width), F32),
             jax.ShapeDtypeStruct((width, hidden), F32),
-            jax.ShapeDtypeStruct((hidden, width), F32),
+            jax.ShapeDtypeStruct((2, hidden // 2, width), F32),
             jax.ShapeDtypeStruct((width, 128), F32),
             jax.ShapeDtypeStruct((hidden // 128, 128), F32),
             jax.ShapeDtypeStruct((width // 128, 128), F32),
             jax.ShapeDtypeStruct((width // 128, 128), F32),
         ),
-        in_specs=[vmem] * 3,
-        out_specs=(vmem,) * 7,
-        compiler_params=pltpu.CompilerParams(vmem_limit_bytes=40 * 2**20),
+        in_specs=[
+            pl.BlockSpec((lines, width), lambda i: (i, 0)),
+            pl.BlockSpec((2, 3, step, 13, 128), lambda i: (0, 0, i, 0, 0)),
+        ],
+        out_specs=(
+            pl.BlockSpec((lines, width), lambda i: (i, 0)),
+            pl.BlockSpec((lines, hidden), lambda i: (i, 0)),
+            pl.BlockSpec((2, lines, width), lambda i: (0, i, 0)),
+            pl.BlockSpec((lines, 128), lambda i: (i, 0)),
+            pl.BlockSpec((hidden // 128, 128), lambda i: (0, 0)),
+            pl.BlockSpec((width // 128, 128), lambda i: (0, 0)),
+            pl.BlockSpec((width // 128, 128), lambda i: (0, 0)),
+        ),
+        compiler_params=pltpu.CompilerParams(vmem_limit_bytes=58 * 2**20),
         name="place_results",
-    )(inc, arr, whole)
-    return (d_prev, d_w1, d_b1.reshape(hidden), d_w2, d_b2.reshape(width), d_c, d_sigma.reshape(width))
+    )(d_prev, sums)
+    return (
+        d_prev, d_w1, d_b1.reshape(hidden), d_w2.reshape(hidden, width), d_b2.reshape(width), d_c, d_sigma.reshape(width),
+    )
 
 
 def solution(mesh):

time: 128 us -> 109 us (0.85)
  Pallas kernels: 123 us -> 108 us
  local copies, waits for them, and re-layouts: 3.98 us -> 0 us
    pallas_call x1, Pallas kernels: 115 us -> 99.7 us  [per_device(): pl.pallas_call(functools.partial(main_kernel, devices), out_shape=(jax.Sh...]
    unnamed x6 -> x0, local copies, waits for them, and re-layouts: 3.98 us -> none
where the time goes in v2:
time: 109 us; the launch traced here: 108 us
  Pallas kernels  108 us (99%)
    pallas_call x1, Pallas kernels, per_device(): pl.pallas_call(functools.partial(main_kernel, devices), out_shape=(jax.Sh...  99.7 us
    pallas_call x1, Pallas kernels, per_device(): pl.pallas_call(finish_kernel, grid=(chips // step,), out_shape=(jax.Shape...  7.92 us

profile of v2, /device:TPU:1, one launch (start us, length us, event | category | flops | bytes accessed | tf_op | source)
XLA Modules:
  0.0 108.3 jit_solution(9840405126668807601)
XLA Ops:
  0.6 99.7 %heun_step.1 = (f32[512,512]{1,0:T(8,128)}, s32[2,3,64,13,128]{4,3,2,1,0:T(8,128)}) custom-call(bf16[512,512]{1,0:T(8,128)(2,1)} %x_hbm.1, s32[1,512]{1,0:T(1,128)} %bitcast.11, s32[1,512]{1,0:T(1,128)} %bitcast.12, bf16[512,512]{1,0:T(8,128)(2,1)} %noise_hbm.1, bf16[512,512]{1,0:T(8,128)(2,1)} %g_hbm.1, bf16[512,128]{1,0:T(8,128)(2,1)} %obs_hbm.1, ...), custom_call_target="tpu_custom_call" | custom-call | tf_op jit(solution)/shard_map/heun_step/pallas_call | solution.py:515
  100.3 7.9 %place_results.1 = (f32[512,512]{1,0:T(8,128)}, f32[512,1024]{1,0:T(8,128)}, f32[2,512,512]{2,1,0:T(8,128)}, f32[512,128]{1,0:T(8,128)}, f32[8,128]{1,0:T(8,128)}, /*index=5*/f32[4,128]{1,0:T(4,128)}, f32[4,128]{1,0:T(4,128)}) custom-call(f32[512,512]{1,0:T(8,128)} %get-tuple-element.16.dp_ref, s32[2,3,64,13,128]{4,3,2,1,0:T(8,128)} %get-tuple-element.17.all_ref), custom_call_target="tpu_custom_call" | custom-call | tf_op jit(solution)/shard_map/place_results/pallas_call | solution.py:577

commit v3 on v2

--- a/solution.py
+++ b/solution.py
@@ -298,6 +298,20 @@
             at = n // 128 + j
             accx[1, 1, at : at + 1, :] = d_b2[:, 128 * j : 128 * (j + 1)]
             accx[1, 2, at : at + 1, :] = d_sigma[:, 128 * j : 128 * (j + 1)]
+    def core_swap(i, source, target):
+        swap = pltpu.make_async_remote_copy(
+            src_ref=source, dst_ref=target, send_sem=ssem.at[8 + i], recv_sem=rsem.at[8 + i],
+            device_id=(other,), device_id_type=MESH,
+        )
+        swap.start()
+        return swap
+
+    theirs = pl.ds((1 - core) * chips, chips)
+    accx[0] = tn(xnb[...], dmean).reshape(chips, 8, 128)
+    for n in range(0, hidden, block):
+        acc2[n // 8 : (n + block) // 8] = tn(aa[:, n : n + block], gf[...]).reshape(block // 8, 8, width)
+
+    swaps = [core_swap(0, acc2.at[theirs], in2)]
     for n in range(0, hidden, block):
         cols = slice(n, n + block)
         zero = nt(gf[rows:, :], w2_ref[cols, :]) * u0[:, cols]
@@ -306,9 +320,17 @@
         for j in range(block // 128):
             at = n // 128 + j
             accx[1, 0, at : at + 1, :] = d_b1[:, 128 * j : 128 * (j + 1)]
+    accx[1, 1, 4:8, :] = jnp.zeros((4, 128), F32)
+    accx[1, 2, 4:8, :] = jnp.zeros((4, 128), F32)
+    accx[1, pl.ds(3, chips - 3)] = jnp.zeros((chips - 3, 8, 128), F32)
+    swaps.append(core_swap(1, accx.at[1 - core], inx))
+    for h in range(2):
+        acc1[h * chips : (h + 1) * chips] = tn(xx[...], gp[:, h * width : (h + 1) * width]).reshape(chips, 8, width)
+    swaps.append(core_swap(2, acc1.at[theirs], in1))
     for n in range(0, width, block):
         cols = slice(n, n + block)
         gxs[:, cols] = gxs[:, cols] + nt(gp[rows:, :], w1_ref[cols, :])
+
 
     gx_high, gx_low = split(gxs[...])
 
@@ -321,29 +343,6 @@
         return carry
 
     lax.fori_loop(0, devices // group, give, 0)
-    exchange(3, ret, arr_ref, True)
-    arr_ref[me] = ret[me]
-
-    accx[1, 1, 4:8, :] = jnp.zeros((4, 128), F32)
-    accx[1, 2, 4:8, :] = jnp.zeros((4, 128), F32)
-    accx[1, pl.ds(3, chips - 3)] = jnp.zeros((chips - 3, 8, 128), F32)
-    accx[0] = tn(xnb[...], dmean).reshape(chips, 8, 128)
-    for n in range(0, hidden, block):
-        acc2[n // 8 : (n + block) // 8] = tn(aa[:, n : n + block], gf[...]).reshape(block // 8, 8, width)
-
-    def core_swap(i, source, target):
-        swap = pltpu.make_async_remote_copy(
-            src_ref=source, dst_ref=target, send_sem=ssem.at[8 + i], recv_sem=rsem.at[8 + i],
-            device_id=(other,), device_id_type=MESH,
-        )
-        swap.start()
-        return swap
-
-    theirs = pl.ds((1 - core) * chips, chips)
-    swaps = [core_swap(0, acc2.at[theirs], in2), core_swap(1, accx.at[1 - core], inx)]
-    for h in range(2):
-        acc1[h * chips : (h + 1) * chips] = tn(xx[...], gp[:, h * width : (h + 1) * width]).reshape(chips, 8, width)
-    swaps.append(core_swap(2, acc1.at[theirs], in1))
     for swap in swaps:
         swap.wait()
 
@@ -375,29 +374,32 @@
                 device_id=(me + (there - coordinate[axis]) * stride[axis],), device_id_type=MESH,
             )
             copy.start()
-            along.append(copy)
-
-    exchange_wait(3, arr_ref)
-
-    def settle(i, carry):
-        at = pl.multiple_of(i * group, group)
-        column = wanted_columns(inc_ref[pl.ds(at, group)])
-        onehot = jnp.where(column == iota((group, MOST, rows), 2).astype(F32), 1.0, 0.0)
-        onehot = onehot.reshape(group * MOST, rows).astype(BF16)
-        word = arr_ref[pl.ds(at, group)]
-        value = decode_wide(word[:, :16], word[:, 16:17]).reshape(group * MOST, width)
-        upper, lower = split(value)
-        return carry + tn(onehot, upper) + tn(onehot, lower)
-
-    dprev[...] = lax.fori_loop(0, devices // group, settle, jnp.zeros((rows, width), F32))
-    settled = pltpu.make_async_copy(dprev, dprev_hbm, lsem.at[7])
-    settled.start()
-
-    for copy in along:
-        copy.wait()
+            along.append((t, copy))
+
+    exchange(3, ret, arr_ref, True)
+    arr_ref[me] = ret[me]
+
     home = [coordinate[axis] * plane for axis, _, _ in streams]
     spot = [coordinate[u] * 4 + coordinate[v] for _, u, v in streams]
+    def over_plane(t, source, target, send_sem, recv_sem):
+        axis, u, v = streams[t]
+        base = core + coordinate[axis] * stride[axis]
+
+        def send(k, carry):
+            there = lax.rem(spot[t] + k, plane)
+            d = base + lax.div(there, 4) * stride[u] + lax.rem(there, 4) * stride[v]
+            pltpu.make_async_remote_copy(
+                src_ref=source(there), dst_ref=target(k), send_sem=send_sem, recv_sem=recv_sem,
+                device_id=(d,), device_id_type=MESH,
+            ).start()
+            return carry
+
+        lax.fori_loop(1, plane, send, 0)
+
     for t in range(3):
+        for stream, copy in along:
+            if stream == t:
+                copy.wait()
 
         def fold(i, carry):
             at = pl.multiple_of(i * step, step)
@@ -409,23 +411,6 @@
             return carry
 
         lax.fori_loop(0, plane // step, fold, 0)
-
-    def over_plane(t, source, target, send_sem, recv_sem):
-        axis, u, v = streams[t]
-        base = core + coordinate[axis] * stride[axis]
-
-        def send(k, carry):
-            there = lax.rem(spot[t] + k, plane)
-            d = base + lax.div(there, 4) * stride[u] + lax.rem(there, 4) * stride[v]
-            pltpu.make_async_remote_copy(
-                src_ref=source(there), dst_ref=target(k), send_sem=send_sem, recv_sem=recv_sem,
-                device_id=(d,), device_id_type=MESH,
-            ).start()
-            return carry
-
-        lax.fori_loop(1, plane, send, 0)
-
-    for t in range(3):
         over_plane(t, lambda there: enc2.at[t, there], lambda k: got2.at[t, k - 1], s2.at[t], r2.at[t])
     for t in range(3):
         bytes_wait(got2.at[t], r2.at[t])
@@ -464,6 +449,22 @@
             copy.start()
             along.append((t, k, copy))
         publish(t, t, home[t])
+    exchange_wait(3, arr_ref)
+
+    def settle(i, carry):
+        at = pl.multiple_of(i * group, group)
+        column = wanted_columns(inc_ref[pl.ds(at, group)])
+        onehot = jnp.where(column == iota((group, MOST, rows), 2).astype(F32), 1.0, 0.0)
+        onehot = onehot.reshape(group * MOST, rows).astype(BF16)
+        word = arr_ref[pl.ds(at, group)]
+        value = decode_wide(word[:, :16], word[:, 16:17]).reshape(group * MOST, width)
+        upper, lower = split(value)
+        return carry + tn(onehot, upper) + tn(onehot, lower)
+
+    dprev[...] = lax.fori_loop(0, devices // group, settle, jnp.zeros((rows, width), F32))
+    settled = pltpu.make_async_copy(dprev, dprev_hbm, lsem.at[7])
+    settled.start()
+
     for t, k, copy in along:
         copy.wait_recv()
         first = lax.rem(coordinate[streams[t][0]] + 4 - k, 4) * plane
@@ -572,7 +573,7 @@
         x_prev, anc_owner.reshape(1, rows), anc_row.reshape(1, rows), noise, g_new, obs,
         w1, b1.reshape(1, hidden), w2, b2.reshape(1, width), c_obs, inv_scale.reshape(1, -1), sigma.reshape(1, width),
     )
-    step = 8
+    step = 32
     lines = step * 8
     d_prev, d_w1, d_w2, d_c, d_b1, d_b2, d_sigma = pl.pallas_call(
         finish_kernel,

time: 109 us -> 102 us (0.936)
  Pallas kernels: 108 us -> 102 us
    pallas_call x1, Pallas kernels: 7.92 us -> 4.72 us  [per_device(): pl.pallas_call(finish_kernel, grid=(chips // step,), out_shape=(jax.Shape...]
    pallas_call x1, Pallas kernels: 99.7 us -> 96.9 us  [per_device(): pl.pallas_call(functools.partial(main_kernel, devices), out_shape=(jax.Sh...]
where the time goes in v3:
time: 102 us
  Pallas kernels  102 us (100%)
    pallas_call x1, Pallas kernels, per_device(): pl.pallas_call(functools.partial(main_kernel, devices), out_shape=(jax.Sh...  96.9 us
    pallas_call x1, Pallas kernels, per_device(): pl.pallas_call(finish_kernel, grid=(chips // step,), out_shape=(jax.Shape...  4.72 us

profile of v3, /device:TPU:1, one launch (start us, length us, event | category | flops | bytes accessed | tf_op | source)
XLA Modules:
  0.0 102.3 jit_solution(1795886130045837111)
XLA Ops:
  0.6 96.9 %heun_step.1 = (f32[512,512]{1,0:T(8,128)}, s32[2,3,64,13,128]{4,3,2,1,0:T(8,128)}) custom-call(bf16[512,512]{1,0:T(8,128)(2,1)} %x_hbm.1, s32[1,512]{1,0:T(1,128)} %bitcast.11, s32[1,512]{1,0:T(1,128)} %bitcast.12, bf16[512,512]{1,0:T(8,128)(2,1)} %noise_hbm.1, bf16[512,512]{1,0:T(8,128)(2,1)} %g_hbm.1, bf16[512,128]{1,0:T(8,128)(2,1)} %obs_hbm.1, ...), custom_call_target="tpu_custom_call" | custom-call | tf_op jit(solution)/shard_map/heun_step/pallas_call | solution.py:516
  97.6 4.7 %place_results.1 = (f32[512,512]{1,0:T(8,128)}, f32[512,1024]{1,0:T(8,128)}, f32[2,512,512]{2,1,0:T(8,128)}, f32[512,128]{1,0:T(8,128)}, f32[8,128]{1,0:T(8,128)}, /*index=5*/f32[4,128]{1,0:T(4,128)}, f32[4,128]{1,0:T(4,128)}) custom-call(f32[512,512]{1,0:T(8,128)} %get-tuple-element.16.dp_ref, s32[2,3,64,13,128]{4,3,2,1,0:T(8,128)} %get-tuple-element.17.all_ref), custom_call_target="tpu_custom_call" | custom-call | tf_op jit(solution)/shard_map/place_results/pallas_call | solution.py:578

commit v4 on v3

--- a/solution.py
+++ b/solution.py
@@ -174,7 +174,7 @@
 
     pl.semaphore_wait(barrier, devices - 1)
 
-    def exchange(stage, source, target, per_partner, by_turn=False):
+    def exchange(stage, source, target, per_partner, by_turn=False, low=1, high=devices):
         def send(k, carry):
             d = lax.rem(me + lax.rem(HOP * k, devices), devices)
             pltpu.make_async_remote_copy(
@@ -187,7 +187,7 @@
             ).start()
             return carry
 
-        lax.fori_loop(1, devices, send, 0)
+        lax.fori_loop(low, high, send, 0)
 
     def exchange_wait(stage, target):
         most = target.at[pl.ds(0, devices - 1)]
@@ -376,7 +376,8 @@
             copy.start()
             along.append((t, copy))
 
-    exchange(3, ret, arr_ref, True)
+    part_one = devices * 5 // 8
+    exchange(3, ret, arr_ref, True, high=part_one)
     arr_ref[me] = ret[me]
 
     home = [coordinate[axis] * plane for axis, _, _ in streams]
@@ -412,6 +413,7 @@
 
         lax.fori_loop(0, plane // step, fold, 0)
         over_plane(t, lambda there: enc2.at[t, there], lambda k: got2.at[t, k - 1], s2.at[t], r2.at[t])
+    exchange(3, ret, arr_ref, True, low=part_one)
     for t in range(3):
         bytes_wait(got2.at[t], r2.at[t])
         value = half[t, spot[t]][None]

time: 102 us -> 100 us (0.980)
  Pallas kernels: 102 us -> 99.6 us
    pallas_call x1, Pallas kernels: 96.9 us -> 94.9 us  [per_device(): pl.pallas_call(functools.partial(main_kernel, devices), out_shape=(jax.Sh...]
where the time goes in v4:
time: 100 us
  Pallas kernels  99.6 us (100%)
    pallas_call x1, Pallas kernels, per_device(): pl.pallas_call(functools.partial(main_kernel, devices), out_shape=(jax.Sh...  94.9 us
    pallas_call x1, Pallas kernels, per_device(): pl.pallas_call(finish_kernel, grid=(chips // step,), out_shape=(jax.Shape...  4.72 us

profile of v4, /device:TPU:1, one launch (start us, length us, event | category | flops | bytes accessed | tf_op | source)
XLA Modules:
  0.0 100.3 jit_solution(16743462895114610962)
XLA Ops:
  0.6 94.9 %heun_step.1 = (f32[512,512]{1,0:T(8,128)}, s32[2,3,64,13,128]{4,3,2,1,0:T(8,128)}) custom-call(bf16[512,512]{1,0:T(8,128)(2,1)} %x_hbm.1, s32[1,512]{1,0:T(1,128)} %bitcast.11, s32[1,512]{1,0:T(1,128)} %bitcast.12, bf16[512,512]{1,0:T(8,128)(2,1)} %noise_hbm.1, bf16[512,512]{1,0:T(8,128)(2,1)} %g_hbm.1, bf16[512,128]{1,0:T(8,128)(2,1)} %obs_hbm.1, ...), custom_call_target="tpu_custom_call" | custom-call | tf_op jit(solution)/shard_map/heun_step/pallas_call | solution.py:518
  95.5 4.7 %place_results.1 = (f32[512,512]{1,0:T(8,128)}, f32[512,1024]{1,0:T(8,128)}, f32[2,512,512]{2,1,0:T(8,128)}, f32[512,128]{1,0:T(8,128)}, f32[8,128]{1,0:T(8,128)}, /*index=5*/f32[4,128]{1,0:T(4,128)}, f32[4,128]{1,0:T(4,128)}) custom-call(f32[512,512]{1,0:T(8,128)} %get-tuple-element.16.dp_ref, s32[2,3,64,13,128]{4,3,2,1,0:T(8,128)} %get-tuple-element.17.all_ref), custom_call_target="tpu_custom_call" | custom-call | tf_op jit(solution)/shard_map/place_results/pallas_call | solution.py:580

commit v5 on v4

--- a/solution.py
+++ b/solution.py
@@ -179,9 +179,9 @@
             d = lax.rem(me + lax.rem(HOP * k, devices), devices)
             pltpu.make_async_remote_copy(
                 src_ref=source.at[d] if per_partner else source.at[0],
-                dst_ref=target.at[k] if by_turn else target.at[me],
+                dst_ref=target.at[devices - k] if by_turn else target.at[me],
                 send_sem=ssem.at[stage],
-                recv_sem=rsem.at[4 + lax.div(k, devices // 4)] if by_turn else rsem.at[stage],
+                recv_sem=rsem.at[stage],
                 device_id=(d,),
                 device_id_type=MESH,
             ).start()
@@ -194,14 +194,14 @@
         bytes_wait(most, ssem.at[stage])
         bytes_wait(most, rsem.at[stage])
 
-    exchange(0, wtab, inc_ref, True)
-    inc_ref[me] = wtab[me]
+    exchange(0, wtab, inc_ref, True, by_turn=True)
+    inc_ref[0] = wtab[me]
     exchange_wait(0, inc_ref)
 
     group = 16
 
     def gather(i, carry):
-        at = pl.multiple_of(i * group, group)
+        at = i * group
         column = wanted_columns(inc_ref[pl.ds(at, group)])
         onehot = jnp.where(column == iota((group, MOST, rows), 2).astype(F32), 1.0, 0.0)
         out = nn(onehot.reshape(group * MOST, rows).astype(BF16), x_ref[...])
@@ -213,15 +213,28 @@
         return carry
 
     loads[0].wait()
-    lax.fori_loop(0, devices // group, gather, 0)
-    exchange(1, send_rows, recv_rows, True, by_turn=True)
-    recv_rows[0] = send_rows[me]
+    quarter = devices // 4
+
+    def send_row(k, carry):
+        pltpu.make_async_remote_copy(
+            src_ref=send_rows.at[k],
+            dst_ref=recv_rows.at[k],
+            send_sem=ssem.at[1],
+            recv_sem=rsem.at[4 + lax.div(k, quarter)],
+            device_id=(lax.rem(me + lax.rem(HOP * k, devices), devices),),
+            device_id_type=MESH,
+        ).start()
+        return carry
+
+    for i in range(devices // group):
+        gather(i, 0)
+        lax.fori_loop(max(1, i * group), (i + 1) * group, send_row, 0)
+    recv_rows[0] = send_rows[0]
     for load in loads[1:]:
         load.wait()
 
     left = jnp.zeros((rows, width // 2), F32)
     right = left
-    quarter = devices // 4
     for i in range(4):
         first = 1 if i == 0 else 0
         bytes_wait(recv_rows.at[pl.ds(0, quarter - first)], rsem.at[4 + i])
@@ -377,8 +390,8 @@
             along.append((t, copy))
 
     part_one = devices * 5 // 8
-    exchange(3, ret, arr_ref, True, high=part_one)
-    arr_ref[me] = ret[me]
+    exchange(3, ret, arr_ref, True, by_turn=True, high=part_one)
+    arr_ref[0] = ret[me]
 
     home = [coordinate[axis] * plane for axis, _, _ in streams]
     spot = [coordinate[u] * 4 + coordinate[v] for _, u, v in streams]
@@ -413,7 +426,7 @@
 
         lax.fori_loop(0, plane // step, fold, 0)
         over_plane(t, lambda there: enc2.at[t, there], lambda k: got2.at[t, k - 1], s2.at[t], r2.at[t])
-    exchange(3, ret, arr_ref, True, low=part_one)
+    exchange(3, ret, arr_ref, True, by_turn=True, low=part_one)
     for t in range(3):
         bytes_wait(got2.at[t], r2.at[t])
         value = half[t, spot[t]][None]

time: 100 us -> 98.2 us (0.982)
  Pallas kernels: 99.6 us -> 97.4 us
    pallas_call x1, Pallas kernels: 94.9 us -> 92.7 us  [per_device(): pl.pallas_call(functools.partial(main_kernel, devices), out_shape=(jax.Sh...]
where the time goes in v5:
time: 98.2 us; the launch traced here: 98 us
  Pallas kernels  97.4 us (99%)
    pallas_call x1, Pallas kernels, per_device(): pl.pallas_call(functools.partial(main_kernel, devices), out_shape=(jax.Sh...  92.7 us
    pallas_call x1, Pallas kernels, per_device(): pl.pallas_call(finish_kernel, grid=(chips // step,), out_shape=(jax.Shape...  4.72 us

profile of v5, /device:TPU:1, one launch (start us, length us, event | category | flops | bytes accessed | tf_op | source)
XLA Modules:
  0.0 98.0 jit_solution(15904587272172728021)
XLA Ops:
  0.6 92.7 %heun_step.1 = (f32[512,512]{1,0:T(8,128)}, s32[2,3,64,13,128]{4,3,2,1,0:T(8,128)}) custom-call(bf16[512,512]{1,0:T(8,128)(2,1)} %x_hbm.1, s32[1,512]{1,0:T(1,128)} %bitcast.11, s32[1,512]{1,0:T(1,128)} %bitcast.12, bf16[512,512]{1,0:T(8,128)(2,1)} %noise_hbm.1, bf16[512,512]{1,0:T(8,128)(2,1)} %g_hbm.1, bf16[512,128]{1,0:T(8,128)(2,1)} %obs_hbm.1, ...), custom_call_target="tpu_custom_call" | custom-call | tf_op jit(solution)/shard_map/heun_step/pallas_call | solution.py:531
  93.3 4.7 %place_results.1 = (f32[512,512]{1,0:T(8,128)}, f32[512,1024]{1,0:T(8,128)}, f32[2,512,512]{2,1,0:T(8,128)}, f32[512,128]{1,0:T(8,128)}, f32[8,128]{1,0:T(8,128)}, /*index=5*/f32[4,128]{1,0:T(4,128)}, f32[4,128]{1,0:T(4,128)}) custom-call(f32[512,512]{1,0:T(8,128)} %get-tuple-element.16.dp_ref, s32[2,3,64,13,128]{4,3,2,1,0:T(8,128)} %get-tuple-element.17.all_ref), custom_call_target="tpu_custom_call" | custom-call | tf_op jit(solution)/shard_map/place_results/pallas_call | solution.py:593

commit v6 on v5

--- a/solution.py
+++ b/solution.py
@@ -213,14 +213,14 @@
         return carry
 
     loads[0].wait()
-    quarter = devices // 4
+    share = devices // 8
 
     def send_row(k, carry):
         pltpu.make_async_remote_copy(
             src_ref=send_rows.at[k],
             dst_ref=recv_rows.at[k],
             send_sem=ssem.at[1],
-            recv_sem=rsem.at[4 + lax.div(k, quarter)],
+            recv_sem=rsem.at[4 + lax.div(k, share)],
             device_id=(lax.rem(me + lax.rem(HOP * k, devices), devices),),
             device_id_type=MESH,
         ).start()
@@ -235,11 +235,11 @@
 
     left = jnp.zeros((rows, width // 2), F32)
     right = left
-    for i in range(4):
+    for i in range(8):
         first = 1 if i == 0 else 0
-        bytes_wait(recv_rows.at[pl.ds(0, quarter - first)], rsem.at[4 + i])
-        block = recv_rows[i * quarter : (i + 1) * quarter].reshape(quarter * 2 * MOST, width // 2)
-        index = (iota((rows, quarter * 2 * MOST), 1) + i * quarter * 2 * MOST).astype(F32)
+        bytes_wait(recv_rows.at[pl.ds(0, share - first)], rsem.at[4 + i])
+        block = recv_rows[i * share : (i + 1) * share].reshape(share * 2 * MOST, width // 2)
+        index = (iota((rows, share * 2 * MOST), 1) + i * share * 2 * MOST).astype(F32)
         take_left = jnp.where(place == index, 1.0, 0.0).astype(BF16)
         take_right = jnp.where(place + MOST == index, 1.0, 0.0).astype(BF16)
         left = left + nn(take_left, block)
@@ -313,7 +313,7 @@
             accx[1, 2, at : at + 1, :] = d_sigma[:, 128 * j : 128 * (j + 1)]
     def core_swap(i, source, target):
         swap = pltpu.make_async_remote_copy(
-            src_ref=source, dst_ref=target, send_sem=ssem.at[8 + i], recv_sem=rsem.at[8 + i],
+            src_ref=source, dst_ref=target, send_sem=ssem.at[8 + i], recv_sem=rsem.at[12 + i],
             device_id=(other,), device_id_type=MESH,
         )
         swap.start()
@@ -578,7 +578,7 @@
             pltpu.VMEM((3, plane - 1, 13, 128), I32),
             pltpu.VMEM((3, 1, 13, 128), I32),
             pltpu.VMEM((3, chips, 13, 128), I32),
-            dma((12,)), dma((12,)), dma((8,)),
+            dma((12,)), dma((16,)), dma((8,)),
             dma((9,)), dma((9,)), dma((3,)), dma((3,)), dma((3,)), dma((3,)), dma((9,)), dma((9,)),
             dma((12,)), dma((12,)), dma((12,)),
         ],

time: 98.2 us -> 98.4 us (level)
  no operation moved by 1% of the time
where the time goes in v6:
time: 98.4 us; the launch traced here: 98.3 us
  Pallas kernels  97.6 us (99%)
    pallas_call x1, Pallas kernels, per_device(): pl.pallas_call(functools.partial(main_kernel, devices), out_shape=(jax.Sh...  92.9 us
    pallas_call x1, Pallas kernels, per_device(): pl.pallas_call(finish_kernel, grid=(chips // step,), out_shape=(jax.Shape...  4.72 us

profile of v6, /device:TPU:1, one launch (start us, length us, event | category | flops | bytes accessed | tf_op | source)
XLA Modules:
  0.0 98.3 jit_solution(5187813938708947624)
XLA Ops:
  0.6 92.9 %heun_step.1 = (f32[512,512]{1,0:T(8,128)}, s32[2,3,64,13,128]{4,3,2,1,0:T(8,128)}) custom-call(bf16[512,512]{1,0:T(8,128)(2,1)} %x_hbm.1, s32[1,512]{1,0:T(1,128)} %bitcast.11, s32[1,512]{1,0:T(1,128)} %bitcast.12, bf16[512,512]{1,0:T(8,128)(2,1)} %noise_hbm.1, bf16[512,512]{1,0:T(8,128)(2,1)} %g_hbm.1, bf16[512,128]{1,0:T(8,128)(2,1)} %obs_hbm.1, ...), custom_call_target="tpu_custom_call" | custom-call | tf_op jit(solution)/shard_map/heun_step/pallas_call | solution.py:531
  93.5 4.7 %place_results.1 = (f32[512,512]{1,0:T(8,128)}, f32[512,1024]{1,0:T(8,128)}, f32[2,512,512]{2,1,0:T(8,128)}, f32[512,128]{1,0:T(8,128)}, f32[8,128]{1,0:T(8,128)}, /*index=5*/f32[4,128]{1,0:T(4,128)}, f32[4,128]{1,0:T(4,128)}) custom-call(f32[512,512]{1,0:T(8,128)} %get-tuple-element.16.dp_ref, s32[2,3,64,13,128]{4,3,2,1,0:T(8,128)} %get-tuple-element.17.all_ref), custom_call_target="tpu_custom_call" | custom-call | tf_op jit(solution)/shard_map/place_results/pallas_call | solution.py:593
